TPU v7x, 32 devices: a whole 2x2x4 slice. The times are simulated.
32 devices in a mesh: gx: 4 (over z), gy: 8 (over y, x, core).
Axes of the slice: x: 2, y: 2, z: 4, core: 2. Of those that a mesh axis runs over, the one named last changes fastest.
Arguments:
- hidden_in: bfloat16 [32, 8192], P(('gx', 'gy')), may hold values from -6 to 6
- norm_gain: float32 [8192], replicated, may hold values from 0.5 to 1.5
- w_query: bfloat16 [8192, 8192], P('gx', 'gy'), may hold values from -0.0625 to 0.0625
- key_weight: bfloat16 [8192, 1024], P('gx', 'gy'), may hold values from -0.375 to 0.375
- value_weight: bfloat16 [8192, 1024], P('gx', 'gy'), may hold values from -0.0625 to 0.0625
- w_output: bfloat16 [8192, 8192], P('gx', 'gy'), may hold values from -0.0625 to 0.0625
- key_cache_units: bfloat16 [32, 2048, 1024], P(('gx', 'gy')), may hold values from -6 to 6
- value_cache_units: bfloat16 [32, 2048, 1024], P(('gx', 'gy')), may hold values from -6 to 6
- key_scale: float32 [32, 16, 8], P(('gx', 'gy')), may hold values from 0.5 to 40
- value_block_scale: float32 [32, 16, 8], P(('gx', 'gy')), may hold values from 0.5 to 2
- lengths: int32 [32], P(('gx', 'gy')), may hold values from 256 to 2048, as said below
Outputs:
- hidden_out: bfloat16 [32, 8192], P(('gx', 'gy'))
Inputs may be any that keep to these rules, and one draw needn't show every extreme that they name: Request r has lengths[r] cached tokens at positions 0 to lengths[r] - 1 of its cache, the new token stands at position lengths[r]; some request has exactly 2048 and some exactly 256.
All inputs are finite; a program needn't handle non-finite values.
Results may differ from a plain program's by a relative error of at most 0.008.
The roundings to bfloat16 on the way count: a program that leaves them out, or rounds other values in their place, can miss the bound.
Values may be sent and summed in bfloat16 or wider, within the bound.
No kernel may reach another device: no remote copies, remote signals or barrier semaphores. Data moves between devices by JAX's collectives and lax.ppermute only.
A program may use at most 64 MiB of HBM per device.

v0:
```python
import math

import jax
import jax.numpy as jnp
from jax import lax
from jax.sharding import PartitionSpec as P

HQ = 64
KEY_VALUE_HEADS = 8
HEAD_SIZE = 128


ROPE_BASE = 500000.0
NORM_EPS = 1e-05
MASKED_SCORE = -1e30


def apply_rotary(values, positions):
    head_dim = values.shape[-1]
    half_dim = head_dim // 2
    freqs = ROPE_BASE ** (-(jnp.arange(half_dim, dtype=jnp.float32) * 2.0) / head_dim)
    angles = positions.astype(jnp.float32)[:, None, None] * freqs
    cosine = jnp.cos(angles)
    sine = jnp.sin(angles)
    wide_vals = values.astype(jnp.float32)
    front_half = wide_vals[..., :half_dim]
    back_half = wide_vals[..., half_dim:]
    joined = jnp.concatenate(
        [front_half * cosine - back_half * sine, back_half * cosine + front_half * sine], axis=-1
    )
    return joined.astype(jnp.bfloat16)


def attend(query, new_key, new_value, keys, values, key_scale, value_block_scale, length):
    heads, head_dim = query.shape
    kv_heads = new_key.shape[0]
    capacity = keys.shape[0]
    group_size = heads // kv_heads
    blocks = key_scale.shape[0]
    inv_root = 1.0 / math.sqrt(head_dim)
    grouped = query.reshape(kv_heads, group_size, head_dim)
    key_rows = keys.reshape(capacity, kv_heads, head_dim)
    value_rows = values.reshape(capacity, kv_heads, head_dim)
    raw_scores = jnp.einsum("gqd,tgd->gqt", grouped, key_rows, preferred_element_type=jnp.float32)
    scaled = (
        raw_scores.reshape(kv_heads, group_size, blocks, capacity // blocks)
        * key_scale.T[:, None, :, None]
    )
    scores = scaled.reshape(kv_heads, group_size, capacity) * inv_root
    live_mask = jnp.arange(capacity) < length
    scores = jnp.where(live_mask, scores, MASKED_SCORE)
    own_score = (
        jnp.einsum("gqd,gd->gq", grouped, new_key, preferred_element_type=jnp.float32) * inv_root
    )
    peak_score = jnp.maximum(jnp.max(scores, axis=-1), own_score)
    probs = jnp.where(live_mask, jnp.exp(scores - peak_score[..., None]), 0.0)
    own_prob = jnp.exp(own_score - peak_score)
    total_weight = jnp.sum(probs, axis=-1) + own_prob
    scaled_probs = (
        probs.reshape(kv_heads, group_size, blocks, capacity // blocks)
        * value_block_scale.T[:, None, :, None]
    )
    weighted = scaled_probs.reshape(kv_heads, group_size, capacity).astype(jnp.bfloat16)
    own_weight = lax.optimization_barrier(own_prob.astype(jnp.bfloat16)).astype(jnp.float32)
    summed = jnp.einsum("gqt,tgd->gqd", weighted, value_rows, preferred_element_type=jnp.float32)
    summed = summed + own_weight[..., None] * new_value.astype(jnp.float32)[:, None, :]
    return (summed / total_weight[..., None]).astype(jnp.bfloat16).reshape(heads * head_dim)


def gather_product(shard_rows, weights):
    local_count, feature_count = shard_rows.shape
    row_groups = lax.axis_size("gx")
    block_width = feature_count // row_groups
    offset = lax.axis_index("gx") * block_width
    columns = lax.dynamic_slice_in_dim(
        lax.all_gather(shard_rows, ("gx", "gy"), axis=0, tiled=True), offset, block_width, 1
    )
    return jnp.concatenate(
        [jnp.dot(columns, weight, preferred_element_type=jnp.float32) for weight in weights], axis=1
    )


def body(
    hidden_in,
    norm_gain,
    w_query,
    key_weight,
    value_weight,
    w_output,
    key_cache_units,
    value_cache_units,
    key_scale,
    value_block_scale,
    lengths,
):
    request_rows = hidden_in.shape[0]
    wide_input = hidden_in.astype(jnp.float32)
    variance = jnp.mean(wide_input * wide_input, axis=1, keepdims=True)
    normed = (wide_input * lax.rsqrt(variance + NORM_EPS) * norm_gain).astype(jnp.bfloat16)
    query_cols = w_query.shape[1]
    key_cols = key_weight.shape[1]
    projected = gather_product(normed, (w_query, key_weight, value_weight))
    summed = lax.psum_scatter(projected, "gx", scatter_dimension=0, tiled=True)
    query_part = summed[:, :query_cols].astype(jnp.bfloat16)
    key_part = summed[:, query_cols : query_cols + key_cols].astype(jnp.bfloat16)
    value_part = summed[:, query_cols + key_cols :].astype(jnp.bfloat16)
    query_full, key_complete, value_complete = (
        lax.all_to_all(query_part, "gy", split_axis=0, concat_axis=1, tiled=True),
        lax.all_to_all(key_part, "gy", split_axis=0, concat_axis=1, tiled=True),
        lax.all_to_all(value_part, "gy", split_axis=0, concat_axis=1, tiled=True),
    )
    query_rot = apply_rotary(query_full.reshape(request_rows, HQ, HEAD_SIZE), lengths)
    key_rotated = apply_rotary(
        key_complete.reshape(request_rows, KEY_VALUE_HEADS, HEAD_SIZE), lengths
    )
    fresh_value = value_complete.reshape(request_rows, KEY_VALUE_HEADS, HEAD_SIZE)
    attended = jax.vmap(attend)(
        query_rot,
        key_rotated,
        fresh_value,
        key_cache_units,
        value_cache_units,
        key_scale,
        value_block_scale,
        lengths,
    )
    update_part = gather_product(attended, (w_output,))
    reduced = lax.psum_scatter(update_part, "gx", scatter_dimension=0, tiled=True)
    update = lax.all_to_all(reduced, "gy", split_axis=0, concat_axis=1, tiled=True)
    return (wide_input + update).astype(jnp.bfloat16)


def solution(mesh):
    placed = (
        P(("gx", "gy"), None),
        P(),
        P("gx", "gy"),
        P("gx", "gy"),
        P("gx", "gy"),
        P("gx", "gy"),
        P(("gx", "gy"), None, None),
        P(("gx", "gy"), None, None),
        P(("gx", "gy"), None, None),
        P(("gx", "gy"), None, None),
        P(("gx", "gy")),
    )
    return jax.shard_map(
        body, mesh=mesh, in_specs=placed, out_specs=P(("gx", "gy"), None), check_vma=False
    )
```

profile of v0, /device:TPU:0, one launch (start us, length us, event | category | flops | bytes accessed | tf_op | source)
XLA Modules:
  0.0 183.8 jit_solution(14603732579346206132)
XLA Ops:
  6.5 1.5 multiply_reduce_fusion
  8.8 0.8 convert_bitcast_fusion
  9.6 46.2 %all-gather = bf16[32,1,8192]{2,1,0:T(2,128)(2,1)S(1)} all-gather(bf16[1,1,8192]{2,1,0:T(2,128)(2,1)S(1)} %convert_bitcast_fusion), channel_id=1, replica_groups=mesh['gx'=4,'gy'=8] {'gx','gy'}, dimensions={0}, use_global_device_ids=true | all-gather | bytes 540672 | tf_op jit(solution)/shard_map/all_gather | solution.py:76
  55.8 0.3 constant_dynamic-slice_fusion.1
  56.1 3.0 %fusion.42 = f32[32,1024]{1,0:T(8,128)S(1)} fusion(bf16[2048,1024]{1,0:T(8,128)(2,1)} %param.13, bf16[32,1,2048]{2,1,0:T(2,128)(2,1)S(1)} %constant_dynamic-slice_fusion.1), kind=kOutput, calls=%fused_computation.57 | convolution fusion | flops 134217728 | bytes 4456448 | tf_op jit(solution)/shard_map/dot_general | solution.py:79
  59.0 0.2 fusion.40
  59.5 0.7 pad_maximum_fusion
  60.9 5.3 %copy.35 = bf16[256,8,8,128]{3,2,1,0:T(8,128)(2,1)} copy(bf16[256,8,8,128]{3,1,2,0:T(8,128)(2,1)} %bitcast.63) | data formatting | bytes 8388608
  66.4 5.3 %copy.36 = bf16[256,8,8,128]{3,2,1,0:T(8,128)(2,1)} copy(bf16[256,8,8,128]{3,1,2,0:T(8,128)(2,1)} %bitcast.64) | data formatting | bytes 8388608
  71.8 4.0 %reduce-scatter.3.cloned.1.call-done = f32[8,1280]{1,0:T(8,128)} async-done(((f32[32,1280]{1,0:T(8,128)}), f32[8,1280]{1,0:T(8,128)}) %reduce-scatter.3.cloned.1.call-update) | async-done | bytes 40976 | tf_op jit(solution)/shard_map/reduce_scatter | solution.py:103
  75.8 0.8 convert.25
  76.6 0.6 copy.25
  77.2 3.6 %all-to-all-start.1 = ((bf16[8,1,128]{2,1,0:T(2,128)(2,1)}), bf16[8,1,128]{2,1,0:T(2,128)(2,1)S(1)}, u32[]{:S(2)}, u32[]{:S(2)}) async-start(bf16[8,1,128]{2,1,0:T(2,128)(2,1)} %copy.25), calls=%async_computation.2 | async-start | bytes 8192 | tf_op jit(solution)/shard_map/all_to_all | solution.py:109
  80.8 0.5 broadcast.97
  81.3 0.7 reduce.5
  81.9 0.6 reshape.241
  82.5 0.6 copy.28
  83.1 2.3 %all-to-all-done.1 = bf16[8,1,128]{2,1,0:T(2,128)(2,1)S(1)} async-done(((bf16[8,1,128]{2,1,0:T(2,128)(2,1)}), bf16[8,1,128]{2,1,0:T(2,128)(2,1)S(1)}, u32[]{:S(2)}, u32[]{:S(2)}) %all-to-all-start.1) | async-done | bytes 2080 | tf_op jit(solution)/shard_map/all_to_all | solution.py:109
  85.4 3.3 %all-to-all-start.2 = ((bf16[8,1,128]{2,1,0:T(2,128)(2,1)}), bf16[8,1,128]{2,1,0:T(2,128)(2,1)S(1)}, u32[]{:S(2)}, u32[]{:S(2)}) async-start(bf16[8,1,128]{2,1,0:T(2,128)(2,1)} %copy.28), calls=%async_computation.3 | async-start | bytes 8192 | tf_op jit(solution)/shard_map/all_to_all | solution.py:110
  88.8 4.5 %all-to-all-done.2 = bf16[8,1,128]{2,1,0:T(2,128)(2,1)S(1)} async-done(((bf16[8,1,128]{2,1,0:T(2,128)(2,1)}), bf16[8,1,128]{2,1,0:T(2,128)(2,1)S(1)}, u32[]{:S(2)}, u32[]{:S(2)}) %all-to-all-start.2) | async-done | bytes 2080 | tf_op jit(solution)/shard_map/all_to_all | solution.py:110
  93.3 3.3 %all-to-all-start = ((bf16[8,2,512]{2,1,0:T(2,128)(2,1)}), bf16[8,2,512]{2,1,0:T(2,128)(2,1)S(1)}, u32[]{:S(2)}, u32[]{:S(2)}) async-start(bf16[8,2,512]{2,1,0:T(2,128)(2,1)} %reshape.241), calls=%async_computation.1 | async-start | bytes 32768 | tf_op jit(solution)/shard_map/all_to_all | solution.py:108
  96.8 4.6 %all-to-all-done = bf16[8,2,512]{2,1,0:T(2,128)(2,1)S(1)} async-done(((bf16[8,2,512]{2,1,0:T(2,128)(2,1)}), bf16[8,2,512]{2,1,0:T(2,128)(2,1)S(1)}, u32[]{:S(2)}, u32[]{:S(2)}) %all-to-all-start) | async-done | bytes 16416 | tf_op jit(solution)/shard_map/all_to_all | solution.py:108
  101.7 3.7 %fusion.43 = (f32[8,8]{1,0:T(8,128)S(1)}, f32[8,8,2048]{2,1,0:T(8,128)S(1)}) fusion(f32[8,2048]{1,0:T(8,128)S(1)} %broadcast_bitcast_fusion.1, bf16[2048,8,128]{2,1,0:T(8,128)(2,1)} %bitcast.62, bf16[8,8,64]{2,1,0:T(8,128)(2,1)S(1)} %get-tuple-element.6, bf16[8,8,64]{2,1,0:T(8,128)(2,1)S(1)} %get-tuple-element.5, pred[2048]{0:T(1024)(128)(4,1)S(1)} %iota_compare_fusion), kind=kOutput, calls=%fused_computation.58 | convolution fusion | flops 34111424 | bytes 4802816 | tf_op jit(solution)/shard_map/vmap(gqd,tgd->gqt)/dot_general | solution.py:44
  105.4 0.2 fusion.22
  105.7 1.2 fusion.19
  106.9 39.7 %all-gather.1 = bf16[32,1,8192]{2,1,0:T(2,128)(2,1)S(1)} all-gather(bf16[1,1,8192]{2,1,0:T(2,128)(2,1)S(1)} %reshape.234), channel_id=1, replica_groups=mesh['gx'=4,'gy'=8] {'gx','gy'}, dimensions={0}, use_global_device_ids=true | all-gather | bytes 540672 | tf_op jit(solution)/shard_map/all_gather | solution.py:76
  146.6 0.3 constant_dynamic-slice_fusion
  146.9 3.6 %fusion.27 = f32[32,1024]{1,0:T(8,128)} fusion(bf16[2048,1024]{1,0:T(8,128)(2,1)} %param.16, bf16[32,1,2048]{2,1,0:T(2,128)(2,1)S(1)} %constant_dynamic-slice_fusion), kind=kOutput, calls=%fused_computation.19 | convolution fusion | flops 134217728 | bytes 4456448 | tf_op jit(solution)/shard_map/dot_general | solution.py:79
  150.5 16.6 %reduce-scatter.5.cloned.1.call-done = f32[8,1024]{1,0:T(8,128)} async-done(((f32[32,1024]{1,0:T(8,128)}), f32[8,1024]{1,0:T(8,128)}) %reduce-scatter.5.cloned.1.call-update) | async-done | bytes 32784 | tf_op jit(solution)/shard_map/reduce_scatter | solution.py:128
  167.2 0.8 copy.30
  168.0 8.3 %all_to_all.55 = f32[8,1,1024]{2,1,0:T(1,128)S(1)} all-to-all(f32[8,1,1024]{2,1,0:T(1,128)S(1)} %copy.30), channel_id=1, replica_groups=mesh['gx'=4,'gy'=8] {'gy'}, dimensions={0} | all-to-all | bytes 65536 | tf_op jit(solution)/shard_map/all_to_all | solution.py:129
  176.3 0.7 add_convert_fusion
  (37 shorter events, 1.2 us)
Async XLA Ops:
  6.5 52.5 %copy-start = (bf16[2048,128]{1,0:T(8,128)(2,1)S(1)}, bf16[2048,128]{1,0:T(8,128)(2,1)}, u32[]{:S(2)}) copy-start(bf16[2048,128]{1,0:T(8,128)(2,1)} %param.15) | copy-start | bytes 1572868
  6.5 52.7 %copy-start.2 = (bf16[2048,128]{1,0:T(8,128)(2,1)S(1)}, bf16[2048,128]{1,0:T(8,128)(2,1)}, u32[]{:S(2)}) copy-start(bf16[2048,128]{1,0:T(8,128)(2,1)} %param.14) | copy-start | bytes 1572868
  6.5 69.2 %reduce-scatter.3.cloned.1.call-start = ((), (), s32[]{:S(2)}) async-start(), calls=%async_computation.6 | async-start | bytes 204800 | tf_op jit(solution)/shard_map/reduce_scatter | solution.py:103
  60.9 5.3 %copy-start.4 = (f32[1,16,8]{1,2,0:T(8,128)S(1)}, f32[1,16,8]{1,2,0:T(8,128)}, u32[]{:S(2)}) copy-start(f32[1,16,8]{1,2,0:T(8,128)} %param.19) | copy-start | bytes 1540
  66.4 5.3 %copy-start.5 = (f32[1,16,8]{1,2,0:T(8,128)S(1)}, f32[1,16,8]{1,2,0:T(8,128)}, u32[]{:S(2)}) copy-start(f32[1,16,8]{1,2,0:T(8,128)} %param.20) | copy-start | bytes 1540
  77.2 8.2 %all-to-all-start.1 = ((bf16[8,1,128]{2,1,0:T(2,128)(2,1)}), bf16[8,1,128]{2,1,0:T(2,128)(2,1)S(1)}, u32[]{:S(2)}, u32[]{:S(2)}) async-start(bf16[8,1,128]{2,1,0:T(2,128)(2,1)} %copy.25), calls=%async_computation.2 | async-start | bytes 8192 | tf_op jit(solution)/shard_map/all_to_all | solution.py:109
  85.4 7.9 %all-to-all-start.2 = ((bf16[8,1,128]{2,1,0:T(2,128)(2,1)}), bf16[8,1,128]{2,1,0:T(2,128)(2,1)S(1)}, u32[]{:S(2)}, u32[]{:S(2)}) async-start(bf16[8,1,128]{2,1,0:T(2,128)(2,1)} %copy.28), calls=%async_computation.3 | async-start | bytes 8192 | tf_op jit(solution)/shard_map/all_to_all | solution.py:110
  93.3 8.0 %all-to-all-start = ((bf16[8,2,512]{2,1,0:T(2,128)(2,1)}), bf16[8,2,512]{2,1,0:T(2,128)(2,1)S(1)}, u32[]{:S(2)}, u32[]{:S(2)}) async-start(bf16[8,2,512]{2,1,0:T(2,128)(2,1)} %reshape.241), calls=%async_computation.1 | async-start | bytes 32768 | tf_op jit(solution)/shard_map/all_to_all | solution.py:108
  96.7 70.5 %reduce-scatter.5.cloned.1.call-start = ((), (), s32[]{:S(2)}) async-start(), calls=%async_computation.7 | async-start | bytes 163840 | tf_op jit(solution)/shard_map/reduce_scatter | solution.py:128
  101.4 4.3 %copy-start.1 = (bf16[256,8,8,128]{3,2,1,0:T(8,128)(2,1)S(1)}, bf16[256,8,8,128]{3,2,1,0:T(8,128)(2,1)}, u32[]{:S(2)}) copy-start(bf16[256,8,8,128]{3,2,1,0:T(8,128)(2,1)} %copy.36) | copy-start | bytes 12582916
  106.9 69.4 %copy-start.3 = (bf16[1,8192]{1,0:T(2,128)(2,1)S(1)}, bf16[1,8192]{1,0:T(2,128)(2,1)}, u32[]{:S(2)}) copy-start(bf16[1,8192]{1,0:T(2,128)(2,1)} %param.11) | copy-start | bytes 49156
Sparse Core Ops, SparseCore 0:
  60.3 15.4 reduce-scatter.2
  150.7 16.4 reduce-scatter.4
where the time goes:
time: 184 us
  blocking collectives  94.2 us (51%)
  waiting for transfers between devices  31.9 us (17%)
  between operations  14.9 us (8%)
  local copies, waits for them, and re-layouts  14.6 us (8%)
  matrix products  12.1 us (7%)
  starting transfers between devices  10.3 us (6%)
  other arithmetic  5.75 us (3%)
    all_gather x2, blocking collectives, gather_product(): lax.all_gather(shard_rows, ('gx', 'gy'), axis=0, tiled=True)  85.9 us
    reduce_scatter x1, waiting for transfers between devices, body(): lax.psum_scatter(update_part, 'gx', scatter_dimension=0, tiled=True)  16.6 us
    unnamed x17, local copies, waits for them, and re-layouts  11.2 us
    all_to_all x1, blocking collectives, body(): lax.all_to_all(reduced, 'gy', split_axis=0, concat_axis=1, tiled=True)  8.3 us
    dot_general x4, matrix products, gather_product(): jnp.dot(columns, weight, preferred_element_type=jnp.float32)  7.02 us
    all_to_all x1, waiting for transfers between devices, body(): lax.all_to_all(query_part, 'gy', split_axis=0, concat_axis=1, tiled=True)  4.55 us
    all_to_all x1, waiting for transfers between devices, body(): lax.all_to_all(value_part, 'gy', split_axis=0, concat_axis=1, tiled=True)  4.49 us
    reduce_scatter x1, waiting for transfers between devices, body(): summed = lax.psum_scatter(projected, 'gx', scatter_dimension=0, tiled=True)  3.98 us
  transfers between devices with their start and end apart: 5, of which 5 were waited for; matrix products, arithmetic and copies ran while one was open for 7% of the time, Pallas kernels for 0%

commit v1 on v0

--- a/solution.py
+++ b/solution.py
@@ -67,17 +67,27 @@
     return (summed / total_weight[..., None]).astype(jnp.bfloat16).reshape(heads * head_dim)
 
 
-def gather_product(shard_rows, weights):
-    local_count, feature_count = shard_rows.shape
-    row_groups = lax.axis_size("gx")
-    block_width = feature_count // row_groups
-    offset = lax.axis_index("gx") * block_width
-    columns = lax.dynamic_slice_in_dim(
-        lax.all_gather(shard_rows, ("gx", "gy"), axis=0, tiled=True), offset, block_width, 1
-    )
-    return jnp.concatenate(
-        [jnp.dot(columns, weight, preferred_element_type=jnp.float32) for weight in weights], axis=1
-    )
+def exchange(blocks):
+    return lax.all_to_all(blocks, ("gx", "gy"), split_axis=0, concat_axis=0, tiled=True)
+
+
+def gather_slices(local_rows):
+    row_groups, column_groups = lax.axis_size("gx"), lax.axis_size("gy")
+    local_count, feature_count = local_rows.shape
+    width = feature_count // row_groups
+    blocks = local_rows.reshape(local_count, row_groups, 1, width // 128, 128).transpose(1, 2, 0, 3, 4)
+    blocks = jnp.broadcast_to(blocks, (row_groups, column_groups) + blocks.shape[2:])
+    blocks = blocks.reshape(-1, local_count, width // 128, 128)
+    return exchange(blocks).reshape(-1, width)
+
+
+def scatter_sums(partial_rows):
+    row_groups, column_groups = lax.axis_size("gx"), lax.axis_size("gy")
+    request_total, columns = partial_rows.shape
+    devices = row_groups * column_groups
+    blocks = partial_rows.reshape(devices, request_total // devices, columns // 128, 128)
+    arrived = exchange(blocks).reshape(row_groups, column_groups, -1, columns)
+    return jnp.sum(arrived, axis=0)
 
 
 def body(
@@ -99,16 +109,18 @@
     normed = (wide_input * lax.rsqrt(variance + NORM_EPS) * norm_gain).astype(jnp.bfloat16)
     query_cols = w_query.shape[1]
     key_cols = key_weight.shape[1]
-    projected = gather_product(normed, (w_query, key_weight, value_weight))
-    summed = lax.psum_scatter(projected, "gx", scatter_dimension=0, tiled=True)
-    query_part = summed[:, :query_cols].astype(jnp.bfloat16)
-    key_part = summed[:, query_cols : query_cols + key_cols].astype(jnp.bfloat16)
-    value_part = summed[:, query_cols + key_cols :].astype(jnp.bfloat16)
-    query_full, key_complete, value_complete = (
-        lax.all_to_all(query_part, "gy", split_axis=0, concat_axis=1, tiled=True),
-        lax.all_to_all(key_part, "gy", split_axis=0, concat_axis=1, tiled=True),
-        lax.all_to_all(value_part, "gy", split_axis=0, concat_axis=1, tiled=True),
+    columns = gather_slices(normed)
+    projected = jnp.concatenate(
+        [
+            jnp.dot(columns, weight, preferred_element_type=jnp.float32)
+            for weight in (w_query, key_weight, value_weight)
+        ],
+        axis=1,
     )
+    summed = scatter_sums(projected).astype(jnp.bfloat16).swapaxes(0, 1)
+    query_full = summed[:, :, :query_cols]
+    key_complete = summed[:, :, query_cols : query_cols + key_cols]
+    value_complete = summed[:, :, query_cols + key_cols :]
     query_rot = apply_rotary(query_full.reshape(request_rows, HQ, HEAD_SIZE), lengths)
     key_rotated = apply_rotary(
         key_complete.reshape(request_rows, KEY_VALUE_HEADS, HEAD_SIZE), lengths
@@ -124,9 +136,8 @@
         value_block_scale,
         lengths,
     )
-    update_part = gather_product(attended, (w_output,))
-    reduced = lax.psum_scatter(update_part, "gx", scatter_dimension=0, tiled=True)
-    update = lax.all_to_all(reduced, "gy", split_axis=0, concat_axis=1, tiled=True)
+    update_part = jnp.dot(gather_slices(attended), w_output, preferred_element_type=jnp.float32)
+    update = scatter_sums(update_part).swapaxes(0, 1).reshape(request_rows, -1)
     return (wide_input + update).astype(jnp.bfloat16)
 
 

time: 184 us -> 74.7 us (0.41)
  blocking collectives: 94.2 us -> 12.2 us
  waiting for transfers between devices: 31.9 us -> 10.2 us
  between operations: 14.9 us -> 1.55 us
  starting transfers between devices: 10.3 us -> 15.7 us
  local copies, waits for them, and re-layouts: 14.6 us -> 18.4 us
    all_gather x2 -> x0, blocking collectives: 85.9 us -> none  [gather_product(): lax.all_gather(shard_rows, ('gx', 'gy'), axis=0, tiled=True)]
    reduce_scatter x2 -> x0, waiting for transfers between devices: 20.6 us -> none  [the longest x1 16.6 us: body(): lax.psum_scatter(update_part, 'gx', scatter_dimension=0, tiled=True)]
    another operation x0 -> x1, local copies, waits for them, and re-layouts: none -> 6.5 us
    all_to_all x3, starting transfers between devices: 10.2 us -> 15.7 us  [exchange(): lax.all_to_all(blocks, ('gx', 'gy'), split_axis=0, concat_axis=0, tiled=T...]
    all_to_all x1, blocking collectives: 8.3 us -> 12.2 us  [exchange(): lax.all_to_all(blocks, ('gx', 'gy'), split_axis=0, concat_axis=0, tiled=T...]
    unnamed x17 -> x15, local copies, waits for them, and re-layouts: 11.2 us -> 8.52 us
    all_to_all x6 -> x0, local copies, waits for them, and re-layouts: 2.5 us -> none  [the longest x1 0.79 us: body(): lax.all_to_all(reduced, 'gy', split_axis=0, concat_axis=1, tiled=True)]
  transfers between devices with their start and end apart: 5 -> 3, of which waited for: 5 -> 2; matrix products, arithmetic and copies ran while one was open for 7% -> 22% of each run, Pallas kernels for 0% -> 0%
where the time goes in v1:
time: 74.7 us; the launch traced here: 74.1 us
  local copies, waits for them, and re-layouts  18.4 us (25%)
  starting transfers between devices  15.7 us (21%)
  blocking collectives  12.2 us (16%)
  matrix products  12.1 us (16%)
  waiting for transfers between devices  10.2 us (14%)
  other arithmetic  4.03 us (5%)
  between operations  1.55 us (2%)
    all_to_all x3, starting transfers between devices, exchange(): lax.all_to_all(blocks, ('gx', 'gy'), split_axis=0, concat_axis=0, tiled=T...  15.7 us
    all_to_all x1, blocking collectives, exchange(): lax.all_to_all(blocks, ('gx', 'gy'), split_axis=0, concat_axis=0, tiled=T...  12.2 us
    all_to_all x3, waiting for transfers between devices, exchange(): lax.all_to_all(blocks, ('gx', 'gy'), split_axis=0, concat_axis=0, tiled=T...  10.2 us
    unnamed x15, local copies, waits for them, and re-layouts  8.52 us
    another operation x1, local copies, waits for them, and re-layouts  6.5 us
    dot_general x1, matrix products, attend(): jnp.einsum('gqd,tgd->gqt', grouped, key_rows, preferred_element_type=jnp....  3.72 us
    dot_general x1, matrix products, body(): jnp.dot(gather_slices(attended), w_output, preferred_element_type=jnp.flo...  3.52 us
    dot_general x3, matrix products, body(): jnp.dot(columns, weight, preferred_element_type=jnp.float32)  3.4 us
  transfers between devices with their start and end apart: 3, of which 2 were waited for; matrix products, arithmetic and copies ran while one was open for 22% of the time, Pallas kernels for 0%

profile of v1, /device:TPU:0, one launch (start us, length us, event | category | flops | bytes accessed | tf_op | source)
XLA Modules:
  0.0 74.1 jit_solution(641527885625497630)
XLA Ops:
  0.0 1.5 %multiply_reduce_fusion = f32[]{:T(128)} fusion(bf16[1,8192]{1,0:T(2,128)(2,1)} %param.11), kind=kLoop, calls=%fused_computation.34 | loop fusion | flops 24575 | bytes 16388 | tf_op jit(solution)/shard_map/reduce_sum | solution.py:108
  2.2 0.9 %convert_reduce_fusion = bf16[8192]{0:T(1024)(128)(2,1)S(1)} fusion(f32[1,8192]{1,0:T(1,128)} %bitcast.88, bf16[1,8192]{1,0:T(2,128)(2,1)} %param.11, f32[]{:T(128)S(6)} %rsqrt.4), kind=kLoop, calls=%fused_computation.33 | loop fusion | flops 32768 | bytes 65540 | tf_op jit(solution)/shard_map/convert_element_type | solution.py:109
  3.1 0.7 broadcast_in_dim.49
  3.7 7.3 %all-to-all-start = ((bf16[32,1,16,128]{3,2,1,0:T(8,128)(2,1)}), bf16[32,1,16,128]{3,2,1,0:T(8,128)(2,1)S(1)}, u32[]{:S(2)}, u32[]{:S(2)}) async-start(bf16[32,1,16,128]{3,2,1,0:T(8,128)(2,1)} %bitcast.2), calls=%async_computation | async-start | bytes 262144 | tf_op jit(solution)/shard_map/all_to_all | solution.py:71
  11.0 0.8 %copy.25 = f32[8,16]{0,1:T(8,128)S(1)} copy(f32[8,16]{1,0:T(8,128)} %bitcast.92) | data formatting | bytes 1024 | tf_op jit(solution)/shard_map/vmap()/mul | solution.py:46
  11.8 0.1 broadcast_bitcast_fusion.1
  12.6 5.4 %copy.34 = bf16[256,8,8,128]{3,2,1,0:T(8,128)(2,1)} copy(bf16[256,8,8,128]{3,1,2,0:T(8,128)(2,1)} %bitcast.76) | data formatting | bytes 8388608
  18.0 3.0 %copy.35 = bf16[256,8,8,128]{3,2,1,0:T(8,128)(2,1)} copy(bf16[256,8,8,128]{3,1,2,0:T(8,128)(2,1)S(1)} %bitcast.77) | data formatting | bytes 8388608
  21.0 0.1 copy.26
  21.2 3.0 %fusion.31 = f32[32,1024]{1,0:T(8,128)S(1)} fusion(bf16[2048,1024]{1,0:T(8,128)(2,1)} %param.13, bf16[4,8,16,128]{3,2,1,0:T(8,128)(2,1)S(1)} %bitcast.80), kind=kOutput, calls=%fused_computation.23 | convolution fusion | flops 134217728 | bytes 4456448 | tf_op jit(solution)/shard_map/dot_general | solution.py:115
  24.2 0.2 fusion.27
  24.4 0.2 fusion.29
  24.6 0.8 %reshape.236 = f32[32,1,10,128]{3,1,2,0:T(1,128)} reshape(f32[32,1280]{1,0:T(8,128)S(1)} %pad_maximum_fusion) | data formatting | bytes 327680 | tf_op jit(solution)/shard_map/reshape | solution.py:88
  25.5 5.8 %all-to-all-start.1 = ((f32[32,1,10,128]{3,1,2,0:T(1,128)}), f32[32,1,10,128]{3,1,2,0:T(1,128)S(1)}, u32[]{:S(2)}, u32[]{:S(2)}) async-start(f32[32,1,10,128]{3,1,2,0:T(1,128)} %reshape.236), calls=%async_computation.1 | async-start | bytes 327680 | tf_op jit(solution)/shard_map/all_to_all | solution.py:71
  31.3 0.1 broadcast_bitcast_fusion
  31.4 8.5 %all-to-all-done.1 = f32[32,1,10,128]{3,1,2,0:T(1,128)S(1)} async-done(((f32[32,1,10,128]{3,1,2,0:T(1,128)}), f32[32,1,10,128]{3,1,2,0:T(1,128)S(1)}, u32[]{:S(2)}, u32[]{:S(2)}) %all-to-all-start.1) | async-done | bytes 163872 | tf_op jit(solution)/shard_map/all_to_all | solution.py:71
  39.9 0.4 reduce.8
  40.4 0.1 fusion.40
  40.5 0.1 fusion.36
  40.6 0.1 maximum_bitcast_fusion
  40.6 0.2 fusion.38
  40.8 3.7 %fusion.49 = (f32[8,8]{1,0:T(8,128)S(1)}, f32[8,8,2048]{2,1,0:T(8,128)S(1)}) fusion(f32[8,2048]{1,0:T(8,128)S(1)} %broadcast_bitcast_fusion.1, bf16[2048,8,128]{2,1,0:T(8,128)(2,1)} %bitcast.74, bf16[8,8,64]{2,1,0:T(8,128)(2,1)S(1)} %get-tuple-element.6, bf16[8,8,64]{2,1,0:T(8,128)(2,1)S(1)} %get-tuple-element.5, pred[2048]{0:T(1024)(128)(4,1)S(1)} %iota_compare_fusion), kind=kOutput, calls=%fused_computation.62 | convolution fusion | flops 34111424 | bytes 4802816 | tf_op jit(solution)/shard_map/vmap(gqd,tgd->gqt)/dot_general | solution.py:44
  44.6 0.2 fusion.22
  44.8 1.2 %fusion.19 = bf16[8,8,128]{2,1,0:T(8,128)(2,1)S(1)} fusion(bf16[2048,8,128]{2,1,0:T(8,128)(2,1)S(1)} %bitcast.79, f32[8,8,2048]{2,1,0:T(8,128)S(1)} %get-tuple-element.14, f32[8,2048]{1,0:T(8,128)S(1)} %broadcast_bitcast_fusion, f32[8,8]{1,0:T(8,128)S(1)} %multiply_maximum_fusion, pred[2048]{0:T(1024)(128)(4,1)S(1)} %iota_compare_fusion, ...), kind=kOutput, calls=%fused_computation.10 | convolution fusion | flops 34111488 | bytes 4807424 | tf_op jit(solution)/shard_map/vmap(gqt,tgd->gqd)/dot_general | solution.py:65
  46.1 0.7 broadcast_in_dim.54
  46.7 2.6 %all-to-all-start.2 = ((bf16[32,1,16,128]{3,2,1,0:T(8,128)(2,1)}), bf16[32,1,16,128]{3,2,1,0:T(8,128)(2,1)S(1)}, u32[]{:S(2)}, u32[]{:S(2)}) async-start(bf16[32,1,16,128]{3,2,1,0:T(8,128)(2,1)} %bitcast.22), calls=%async_computation.2 | async-start | bytes 262144 | tf_op jit(solution)/shard_map/all_to_all | solution.py:71
  49.3 6.5 %copy.32 = bf16[1024,2048]{1,0:T(8,128)(2,1)} copy(bf16[1024,2048]{0,1:T(8,128)(2,1)} %bitcast.78) | data formatting | bytes 8388608 | tf_op jit(solution)/shard_map/reshape.160
  55.8 1.7 %all-to-all-done.2 = bf16[32,1,16,128]{3,2,1,0:T(8,128)(2,1)S(1)} async-done(((bf16[32,1,16,128]{3,2,1,0:T(8,128)(2,1)}), bf16[32,1,16,128]{3,2,1,0:T(8,128)(2,1)S(1)}, u32[]{:S(2)}, u32[]{:S(2)}) %all-to-all-start.2) | async-done | bytes 131104 | tf_op jit(solution)/shard_map/all_to_all | solution.py:71
  57.6 3.5 %convolution_bitcast_fusion = f32[32,1,8,128]{3,0,2,1:T(8,128)S(1)} fusion(bf16[32,2048,1]{1,0,2:T(8,128)(2,1)S(1)} %reshape.235, bf16[8,128,2048]{2,1,0:T(8,128)(2,1)} %bitcast.75), kind=kOutput, calls=%fused_computation.7 | convolution fusion | flops 134217728 | bytes 4456448 | tf_op jit(solution)/shard_map/dot_general | solution.py:139
  61.1 0.1 copy.29
  61.2 12.2 %all_to_all.20 = f32[32,1,8,128]{3,2,1,0:T(8,128)S(1)} all-to-all(f32[32,1,8,128]{3,2,1,0:T(8,128)S(1)} %copy.29), channel_id=1, replica_groups=mesh['gx'=4,'gy'=8] {'gx','gy'}, dimensions={0} | all-to-all | bytes 262144 | tf_op jit(solution)/shard_map/all_to_all | solution.py:71
  73.5 0.7 add_convert_fusion
  (28 shorter events, 0.3 us)
Async XLA Ops:
  0.0 24.2 %copy-start = (bf16[2048,128]{1,0:T(8,128)(2,1)S(1)}, bf16[2048,128]{1,0:T(8,128)(2,1)}, u32[]{:S(2)}) copy-start(bf16[2048,128]{1,0:T(8,128)(2,1)} %param.15) | copy-start | bytes 1572868
  3.7 17.4 %all-to-all-start = ((bf16[32,1,16,128]{3,2,1,0:T(8,128)(2,1)}), bf16[32,1,16,128]{3,2,1,0:T(8,128)(2,1)S(1)}, u32[]{:S(2)}, u32[]{:S(2)}) async-start(bf16[32,1,16,128]{3,2,1,0:T(8,128)(2,1)} %bitcast.2), calls=%async_computation | async-start | bytes 262144 | tf_op jit(solution)/shard_map/all_to_all | solution.py:71
  12.5 5.5 %copy-start.1 = (bf16[1,2048,1024]{2,1,0:T(8,128)(2,1)S(1)}, bf16[1,2048,1024]{2,1,0:T(8,128)(2,1)}, u32[]{:S(2)}) copy-start(bf16[1,2048,1024]{2,1,0:T(8,128)(2,1)} %param.18) | copy-start | bytes 12582916
  18.0 3.0 %copy-start.5 = (f32[1,16,8]{1,2,0:T(8,128)S(1)}, f32[1,16,8]{1,2,0:T(8,128)}, u32[]{:S(2)}) copy-start(f32[1,16,8]{1,2,0:T(8,128)} %param.20) | copy-start | bytes 1540
  21.0 3.4 %copy-start.3 = (bf16[2048,128]{1,0:T(8,128)(2,1)S(1)}, bf16[2048,128]{1,0:T(8,128)(2,1)}, u32[]{:S(2)}) copy-start(bf16[2048,128]{1,0:T(8,128)(2,1)} %param.14) | copy-start | bytes 1572868
  25.5 14.4 %all-to-all-start.1 = ((f32[32,1,10,128]{3,1,2,0:T(1,128)}), f32[32,1,10,128]{3,1,2,0:T(1,128)S(1)}, u32[]{:S(2)}, u32[]{:S(2)}) async-start(f32[32,1,10,128]{3,1,2,0:T(1,128)} %reshape.236), calls=%async_computation.1 | async-start | bytes 327680 | tf_op jit(solution)/shard_map/all_to_all | solution.py:71
  40.4 4.4 %copy-start.2 = (bf16[256,8,8,128]{3,2,1,0:T(8,128)(2,1)S(1)}, bf16[256,8,8,128]{3,2,1,0:T(8,128)(2,1)}, u32[]{:S(2)}) copy-start(bf16[256,8,8,128]{3,2,1,0:T(8,128)(2,1)} %copy.35) | copy-start | bytes 12582916
  46.7 10.8 %all-to-all-start.2 = ((bf16[32,1,16,128]{3,2,1,0:T(8,128)(2,1)}), bf16[32,1,16,128]{3,2,1,0:T(8,128)(2,1)S(1)}, u32[]{:S(2)}, u32[]{:S(2)}) async-start(bf16[32,1,16,128]{3,2,1,0:T(8,128)(2,1)} %bitcast.22), calls=%async_computation.2 | async-start | bytes 262144 | tf_op jit(solution)/shard_map/all_to_all | solution.py:71
  55.8 17.6 %copy-start.4 = (bf16[1,8192]{1,0:T(2,128)(2,1)S(1)}, bf16[1,8192]{1,0:T(2,128)(2,1)}, u32[]{:S(2)}) copy-start(bf16[1,8192]{1,0:T(2,128)(2,1)} %param.11) | copy-start | bytes 49156

commit v2 on v0

v2 whole, which is shorter than its diff:
```python
import functools
import math

import jax
import jax.numpy as jnp
from jax import lax
from jax.experimental import pallas as pl
from jax.experimental.pallas import tpu as pltpu
from jax.sharding import PartitionSpec as P

HQ = 64
KEY_VALUE_HEADS = 8
HEAD_SIZE = 128
GROUP = HQ // KEY_VALUE_HEADS

ROPE_BASE = 500000.0
NORM_EPS = 1e-05
MASKED_SCORE = -1e30

LANES = 128
VMEM = pl.BlockSpec(memory_space=pltpu.VMEM)
SMEM = pl.BlockSpec(memory_space=pltpu.SMEM)
PARAMS = pltpu.CompilerParams(vmem_limit_bytes=24 * 1024 * 1024)


def exchange(blocks):
    return lax.all_to_all(blocks, ("gx", "gy"), split_axis=0, concat_axis=0, tiled=True)


def in_vmem(array):
    return pltpu.with_memory_space_constraint(array, pltpu.VMEM)


def norm_kernel(row_groups, hidden_ref, gain_ref, blocks_ref, wide_ref):
    rows = wide_ref.shape[0]
    for row in range(rows):
        wide_ref[row : row + 1, :] = hidden_ref[:, row * LANES : (row + 1) * LANES].astype(
            jnp.float32
        )
    wide = wide_ref[...]
    variance = jnp.sum(wide * wide, keepdims=True) * (1.0 / (rows * LANES))
    normed = (wide * lax.rsqrt(variance + NORM_EPS) * gain_ref[...]).astype(jnp.bfloat16)
    spread_blocks(normed, row_groups, blocks_ref)


def spread_blocks(rows, row_groups, blocks_ref):
    per_block = rows.shape[0] // row_groups
    column_groups = blocks_ref.shape[0] // row_groups
    for i in range(row_groups):
        part = rows[i * per_block : (i + 1) * per_block]
        for j in range(column_groups):
            blocks_ref[i * column_groups + j] = part


def flat_rows(blocks_ref):
    return jnp.concatenate([blocks_ref[:, k, :] for k in range(blocks_ref.shape[1])], axis=1)


def send_rows(product, out_ref):
    requests, columns = product.shape
    count = columns // LANES
    for n in range(count):
        out_ref[pl.ds(n, requests, stride=count), :] = product[:, n * LANES : (n + 1) * LANES]


def project_kernel(blocks_ref, w_query_ref, key_ref, value_ref, out_ref):
    rows = flat_rows(blocks_ref)
    send_rows(
        jnp.concatenate(
            [
                jnp.dot(rows, ref[...], preferred_element_type=jnp.float32)
                for ref in (w_query_ref, key_ref, value_ref)
            ],
            axis=1,
        ),
        out_ref,
    )


def output_kernel(blocks_ref, weight_ref, out_ref):
    rows = flat_rows(blocks_ref)
    send_rows(jnp.dot(rows, weight_ref[...], preferred_element_type=jnp.float32), out_ref)


def attend_kernel(
    row_groups,
    length_ref,
    key_scale_ref,
    value_scale_ref,
    turn_ref,
    sums_ref,
    keys_ref,
    values_ref,
    blocks_ref,
    score_ref,
    result_ref,
):
    length = length_ref[0]
    capacity = keys_ref.shape[0]
    scale_blocks = key_scale_ref.shape[1]
    block = capacity // scale_blocks
    inv_root = 1.0 / math.sqrt(HEAD_SIZE)
    per_group = GROUP + 2
    cosine, sine = turn_ref[0:1, :], turn_ref[1:2, :]

    def rotate(wide):
        return (wide * cosine + pltpu.roll(wide, HEAD_SIZE // 2, 1) * sine).astype(jnp.bfloat16)

    def summed(first, count):
        total = sums_ref[first : first + count, :]
        for i in range(1, row_groups):
            start = i * KEY_VALUE_HEADS * per_group + first
            total = total + sums_ref[start : start + count, :]
        return total.astype(jnp.bfloat16).astype(jnp.float32)

    positions = lax.broadcasted_iota(jnp.int32, (1, capacity), 1)
    live = positions < length
    queries, own_scores, new_values = [], [], []
    for g in range(KEY_VALUE_HEADS):
        query = rotate(summed(g * per_group, GROUP))
        new_key = rotate(summed(g * per_group + GROUP, 1))
        new_values.append(summed(g * per_group + GROUP + 1, 1))
        own_scores.append(
            jnp.sum(
                query.astype(jnp.float32) * new_key.astype(jnp.float32), axis=1, keepdims=True
            )
            * inv_root
        )
        queries.append(query)
    for g in range(KEY_VALUE_HEADS):
        raw = lax.dot_general(
            queries[g],
            keys_ref[:, g * HEAD_SIZE : (g + 1) * HEAD_SIZE],
            (((1,), (1,)), ((), ())),
            preferred_element_type=jnp.float32,
        )
        for b in range(scale_blocks):
            span = slice(b * block, (b + 1) * block)
            scaled = raw[:, span] * key_scale_ref[g, b] * inv_root
            score_ref[g * GROUP : (g + 1) * GROUP, span] = jnp.where(
                live[:, span], scaled, MASKED_SCORE
            )
    for g in range(KEY_VALUE_HEADS):
        heads = slice(g * GROUP, (g + 1) * GROUP)
        scores = score_ref[heads, :]
        peak = jnp.maximum(jnp.max(scores, axis=1, keepdims=True), own_scores[g])
        probs = jnp.where(live, jnp.exp(scores - peak), 0.0)
        own_prob = jnp.exp(own_scores[g] - peak)
        total = jnp.sum(probs, axis=1, keepdims=True) + own_prob
        weighted = jnp.concatenate(
            [
                (probs[:, b * block : (b + 1) * block] * value_scale_ref[g, b]).astype(jnp.bfloat16)
                for b in range(scale_blocks)
            ],
            axis=1,
        )
        own_weight = own_prob.astype(jnp.bfloat16).astype(jnp.float32)
        sums = jnp.dot(
            weighted,
            values_ref[:, g * HEAD_SIZE : (g + 1) * HEAD_SIZE],
            preferred_element_type=jnp.float32,
        )
        result_ref[heads, :] = (sums + own_weight * new_values[g]) / total
    spread_blocks(result_ref[...].astype(jnp.bfloat16), row_groups, blocks_ref)


def rotation_rows(position):
    half = HEAD_SIZE // 2
    freqs = ROPE_BASE ** (-(jnp.arange(half, dtype=jnp.float32) * 2.0) / HEAD_SIZE)
    angles = position.astype(jnp.float32) * freqs
    cosine, sine = jnp.cos(angles), jnp.sin(angles)
    return jnp.stack([jnp.concatenate([cosine, cosine]), jnp.concatenate([-sine, sine])])


def body(
    hidden_in,
    norm_gain,
    w_query,
    key_weight,
    value_weight,
    w_output,
    key_cache_units,
    value_cache_units,
    key_scale,
    value_block_scale,
    lengths,
):
    row_groups, column_groups = lax.axis_size("gx"), lax.axis_size("gy")
    devices = row_groups * column_groups
    width = hidden_in.shape[1]
    slice_rows = width // row_groups // LANES
    query_cols, key_cols = w_query.shape[1], key_weight.shape[1]
    out_cols = w_output.shape[1]
    blocks_type = jax.ShapeDtypeStruct((devices, slice_rows, LANES), jnp.bfloat16)

    blocks = pl.pallas_call(
        functools.partial(norm_kernel, row_groups),
        out_shape=blocks_type,
        in_specs=[VMEM, VMEM],
        out_specs=VMEM,
        scratch_shapes=[pltpu.VMEM((width // LANES, LANES), jnp.float32)],
        compiler_params=PARAMS,
    )(hidden_in, norm_gain.reshape(-1, LANES))
    turn = rotation_rows(lengths[0])

    sent_rows = (query_cols + 2 * key_cols) // LANES
    partial = pl.pallas_call(
        project_kernel,
        out_shape=jax.ShapeDtypeStruct((devices * sent_rows, LANES), jnp.float32),
        in_specs=[VMEM] * 4,
        out_specs=VMEM,
        compiler_params=PARAMS,
    )(exchange(blocks), in_vmem(w_query), in_vmem(key_weight), in_vmem(value_weight))
    sums = exchange(partial.reshape(devices, sent_rows, 1, LANES))
    if key_cols != HEAD_SIZE:
        sums = sums.reshape(row_groups, column_groups, sent_rows * LANES)
        sums = jnp.concatenate(
            [
                part.reshape(row_groups, KEY_VALUE_HEADS, -1, HEAD_SIZE)
                for part in jnp.split(sums, (query_cols, query_cols + key_cols), axis=2)
            ],
            axis=2,
        )
    sums = sums.reshape(-1, LANES)

    attended = pl.pallas_call(
        functools.partial(attend_kernel, row_groups),
        out_shape=blocks_type,
        in_specs=[SMEM, SMEM, SMEM, VMEM, VMEM, VMEM, VMEM],
        out_specs=VMEM,
        scratch_shapes=[
            pltpu.VMEM((HQ, key_cache_units.shape[1]), jnp.float32),
            pltpu.VMEM((HQ, HEAD_SIZE), jnp.float32),
        ],
        compiler_params=PARAMS,
    )(
        lengths,
        key_scale[0].T,
        value_block_scale[0].T,
        turn,
        sums,
        in_vmem(key_cache_units[0]),
        in_vmem(value_cache_units[0]),
    )

    out_rows = out_cols // LANES
    partial = pl.pallas_call(
        output_kernel,
        out_shape=jax.ShapeDtypeStruct((devices * out_rows, LANES), jnp.float32),
        in_specs=[VMEM] * 2,
        out_specs=VMEM,
        compiler_params=PARAMS,
    )(exchange(attended), in_vmem(w_output))
    update = exchange(partial.reshape(devices, out_rows, LANES))
    update = jnp.sum(update.reshape(row_groups, column_groups * out_rows, LANES), axis=0)
    return (hidden_in.astype(jnp.float32) + update.reshape(1, width)).astype(jnp.bfloat16)


def solution(mesh):
    placed = (
        P(("gx", "gy"), None),
        P(),
        P("gx", "gy"),
        P("gx", "gy"),
        P("gx", "gy"),
        P("gx", "gy"),
        P(("gx", "gy"), None, None),
        P(("gx", "gy"), None, None),
        P(("gx", "gy"), None, None),
        P(("gx", "gy"), None, None),
        P(("gx", "gy")),
    )
    return jax.shard_map(
        body, mesh=mesh, in_specs=placed, out_specs=P(("gx", "gy"), None), check_vma=False
    )
```

time: 184 us -> 64.8 us (0.35)
  blocking collectives: 94.2 us -> 20.3 us
  waiting for transfers between devices: 31.9 us -> 15.9 us
  between operations: 14.9 us -> 0.72 us
  matrix products: 12.1 us -> 0 us
  Pallas kernels: 0 us -> 6.33 us
  other arithmetic: 5.75 us -> 0.94 us
  local copies, waits for them, and re-layouts: 14.6 us -> 10.2 us
    all_gather x2 -> x0, blocking collectives: 85.9 us -> none  [gather_product(): lax.all_gather(shard_rows, ('gx', 'gy'), axis=0, tiled=True)]
    reduce_scatter x2 -> x0, waiting for transfers between devices: 20.6 us -> none  [the longest x1 16.6 us: body(): lax.psum_scatter(update_part, 'gx', scatter_dimension=0, tiled=True)]
    dot_general x7 -> x0, matrix products: 12.1 us -> none  [the longest x4 7.02 us: gather_product(): jnp.dot(columns, weight, preferred_element_type=jnp.float32)]
    all_to_all x1 -> x2, blocking collectives: 8.3 us -> 20.3 us  [exchange(): lax.all_to_all(blocks, ('gx', 'gy'), split_axis=0, concat_axis=0, tiled=T...]
    pallas_call x0 -> x4, Pallas kernels: none -> 6.33 us  [the longest x1 2.98 us: body(): pl.pallas_call(functools.partial(attend_kernel, row_groups), out_shape=bl...]
    all_to_all x3 -> x2, waiting for transfers between devices: 11.3 us -> 15.9 us  [exchange(): lax.all_to_all(blocks, ('gx', 'gy'), split_axis=0, concat_axis=0, tiled=T...]
    all_to_all x6 -> x0, local copies, waits for them, and re-layouts: 2.5 us -> none  [the longest x1 0.79 us: body(): lax.all_to_all(reduced, 'gy', split_axis=0, concat_axis=1, tiled=True)]
    unnamed x17 -> x22, local copies, waits for them, and re-layouts: 11.2 us -> 10.2 us
  transfers between devices with their start and end apart: 5 -> 2, of which waited for: 5 -> 2; matrix products, arithmetic and copies ran while one was open for 7% -> 0% of each run, Pallas kernels for 0% -> 0%
where the time goes in v2:
time: 64.8 us; the launch traced here: 64.2 us
  blocking collectives  20.3 us (31%)
  waiting for transfers between devices  15.9 us (25%)
  local copies, waits for them, and re-layouts  10.2 us (16%)
  starting transfers between devices  9.87 us (15%)
  Pallas kernels  6.33 us (10%)
  other arithmetic  0.94 us (1%)
  between operations  0.72 us (1%)
    all_to_all x2, blocking collectives, exchange(): lax.all_to_all(blocks, ('gx', 'gy'), split_axis=0, concat_axis=0, tiled=T...  20.3 us
    all_to_all x2, waiting for transfers between devices, exchange(): lax.all_to_all(blocks, ('gx', 'gy'), split_axis=0, concat_axis=0, tiled=T...  15.9 us
    unnamed x22, local copies, waits for them, and re-layouts  10.2 us
    all_to_all x2, starting transfers between devices, exchange(): lax.all_to_all(blocks, ('gx', 'gy'), split_axis=0, concat_axis=0, tiled=T...  9.87 us
    pallas_call x1, Pallas kernels, body(): pl.pallas_call(functools.partial(attend_kernel, row_groups), out_shape=bl...  2.98 us
    pallas_call x1, Pallas kernels, body(): pl.pallas_call(project_kernel, out_shape=jax.ShapeDtypeStruct((devices *...  1.67 us
  transfers between devices with their start and end apart: 2, of which 2 were waited for; matrix products, arithmetic and copies ran while one was open for 0% of the time, Pallas kernels for 0%

profile of v2, /device:TPU:0, one launch (start us, length us, event | category | flops | bytes accessed | tf_op | source)
XLA Modules:
  0.0 64.2 jit_solution(4196345960574456909)
XLA Ops:
  0.0 0.8 %copy-done.6 = bf16[1,8192]{1,0:T(2,128)(2,1)S(1)} copy-done((bf16[1,8192]{1,0:T(2,128)(2,1)S(1)}, bf16[1,8192]{1,0:T(2,128)(2,1)}, u32[]{:S(2)}) %copy-start.6) | copy-done | bytes 16408
  0.8 0.0 copy-start.8
  0.8 0.8 %copy-done.8 = f32[8192]{0:T(1024)S(1)} copy-done((f32[8192]{0:T(1024)S(1)}, f32[8192]{0:T(1024)}, u32[]{:S(2)}) %copy-start.8) | copy-done | bytes 32792
  1.5 0.0 copy-start.9
  1.5 0.0 copy-start.10
  1.5 0.8 %shard_map.109 = bf16[32,16,128]{2,1,0:T(8,128)(2,1)} custom-call(bf16[1,8192]{1,0:T(2,128)(2,1)S(1)} %copy-done.6, f32[64,128]{1,0:T(8,128)S(1)} %bitcast.25), custom_call_target="tpu_custom_call" | custom-call | tf_op jit(solution)/shard_map/pallas_call | solution.py:196
  2.3 7.3 %all-to-all-start = ((bf16[32,16,128]{2,1,0:T(8,128)(2,1)}), bf16[32,16,128]{2,1,0:T(8,128)(2,1)S(1)}, u32[]{:S(2)}, u32[]{:S(2)}) async-start(bf16[32,16,128]{2,1,0:T(8,128)(2,1)} %shard_map.109), calls=%async_computation | async-start | bytes 262144 | tf_op jit(solution)/shard_map/all_to_all | solution.py:27
  10.3 0.1 fusion.2
  10.3 0.1 fusion
  10.4 7.5 %all-to-all-done.blocks_ref = bf16[32,16,128]{2,1,0:T(8,128)(2,1)S(1)} async-done(((bf16[32,16,128]{2,1,0:T(8,128)(2,1)}), bf16[32,16,128]{2,1,0:T(8,128)(2,1)S(1)}, u32[]{:S(2)}, u32[]{:S(2)}) %all-to-all-start) | async-done | bytes 131104 | tf_op jit(solution)/shard_map/all_to_all | solution.py:27
  17.9 0.0 copy-start
  17.9 2.2 %copy-done = bf16[2048,1024]{1,0:T(8,128)(2,1)S(1)} copy-done((bf16[2048,1024]{1,0:T(8,128)(2,1)S(1)}, bf16[2048,1024]{1,0:T(8,128)(2,1)}, u32[]{:S(2)}) %copy-start) | copy-done | bytes 4194328
  20.1 0.0 copy-start.4
  20.1 1.0 %copy-done.4 = bf16[2048,128]{1,0:T(8,128)(2,1)S(1)} copy-done((bf16[2048,128]{1,0:T(8,128)(2,1)S(1)}, bf16[2048,128]{1,0:T(8,128)(2,1)}, u32[]{:S(2)}) %copy-start.4) | copy-done | bytes 524312
  21.1 1.0 %copy-done.5 = bf16[2048,128]{1,0:T(8,128)(2,1)S(1)} copy-done((bf16[2048,128]{1,0:T(8,128)(2,1)S(1)}, bf16[2048,128]{1,0:T(8,128)(2,1)}, u32[]{:S(2)}) %copy-start.5) | copy-done | bytes 524312
  22.1 1.7 %shard_map.110 = f32[320,128]{1,0:T(8,128)} custom-call(bf16[32,16,128]{2,1,0:T(8,128)(2,1)S(1)} %all-to-all-done.blocks_ref, bf16[2048,1024]{1,0:T(8,128)(2,1)S(1)} %copy-done, bf16[2048,128]{1,0:T(8,128)(2,1)S(1)} %copy-done.4, bf16[2048,128]{1,0:T(8,128)(2,1)S(1)} %copy-done.5), custom_call_target="tpu_custom_call" | custom-call | tf_op jit(solution)/shard_map/pallas_call | solution.py:207
  23.8 2.6 %all-to-all-start.1 = ((f32[32,10,1,128]{3,2,1,0:T(1,128)}), f32[32,10,1,128]{3,2,1,0:T(1,128)S(1)}, u32[]{:S(2)}, u32[]{:S(2)}) async-start(f32[32,10,1,128]{3,2,1,0:T(1,128)} %bitcast.8), calls=%async_computation.1 | async-start | bytes 327680 | tf_op jit(solution)/shard_map/all_to_all | solution.py:27
  26.4 0.1 maximum_bitcast_fusion
  26.5 0.1 maximum_bitcast_fusion.1
  26.6 8.4 %all-to-all-done.1 = f32[32,10,1,128]{3,2,1,0:T(1,128)S(1)} async-done(((f32[32,10,1,128]{3,2,1,0:T(1,128)}), f32[32,10,1,128]{3,2,1,0:T(1,128)S(1)}, u32[]{:S(2)}, u32[]{:S(2)}) %all-to-all-start.1) | async-done | bytes 163872 | tf_op jit(solution)/shard_map/all_to_all | solution.py:27
  35.0 0.0 copy-done.9
  35.0 0.0 copy-done.10
  35.0 2.2 %copy-done.1 = bf16[1,2048,1024]{2,1,0:T(8,128)(2,1)S(1)} copy-done((bf16[1,2048,1024]{2,1,0:T(8,128)(2,1)S(1)}, bf16[1,2048,1024]{2,1,0:T(8,128)(2,1)}, u32[]{:S(2)}) %copy-start.1) | copy-done | bytes 4194328
  37.2 2.2 %copy-done.2 = bf16[1,2048,1024]{2,1,0:T(8,128)(2,1)S(1)} copy-done((bf16[1,2048,1024]{2,1,0:T(8,128)(2,1)S(1)}, bf16[1,2048,1024]{2,1,0:T(8,128)(2,1)}, u32[]{:S(2)}) %copy-start.2) | copy-done | bytes 4194328
  39.4 3.0 %shard_map.111 = bf16[32,16,128]{2,1,0:T(8,128)(2,1)S(1)} custom-call(s32[1]{0:T(128)S(6)} %copy.13.length_ref, f32[8,16]{1,0:T(8,128)S(1)} %bitcast.26, f32[8,16]{1,0:T(8,128)S(1)} %bitcast.27, f32[2,128]{1,0:T(2,128)S(1)} %pad_maximum_fusion.turn_ref, f32[320,128]{1,0:T(8,128)S(1)} %bitcast.23, bf16[2048,1024]{1,0:T(8,128)(2,1)S(1)} %bitcast.21, ...), custom_call_target="tpu_custom_call" | custom-call | tf_op jit(solution)/shard_map/pallas_call | solution.py:226
  42.3 0.0 copy-start.7
  42.4 10.3 %all_to_all.20.blocks_ref = bf16[32,16,128]{2,1,0:T(8,128)(2,1)S(1)} all-to-all(bf16[32,16,128]{2,1,0:T(8,128)(2,1)S(1)} %shard_map.111), channel_id=1, replica_groups=mesh['gx'=4,'gy'=8] {'gx','gy'}, dimensions={0} | all-to-all | bytes 262144 | tf_op jit(solution)/shard_map/all_to_all | solution.py:27
  52.6 0.0 copy-done.3
  52.6 0.9 %shard_map.112 = f32[256,128]{1,0:T(8,128)S(1)} custom-call(bf16[32,16,128]{2,1,0:T(8,128)(2,1)S(1)} %all_to_all.20.blocks_ref, bf16[2048,1024]{1,0:T(8,128)(2,1)S(1)} %copy-done.3), custom_call_target="tpu_custom_call" | custom-call | tf_op jit(solution)/shard_map/pallas_call | solution.py:247
  53.5 10.0 %all_to_all.21 = f32[32,8,128]{2,1,0:T(8,128)S(1)} all-to-all(f32[32,8,128]{2,1,0:T(8,128)S(1)} %bitcast.24), channel_id=1, replica_groups=mesh['gx'=4,'gy'=8] {'gx','gy'}, dimensions={0} | all-to-all | bytes 262144 | tf_op jit(solution)/shard_map/all_to_all | solution.py:27
  63.5 0.0 copy-done.7
  63.5 0.7 %add_convert_fusion = bf16[1,8192]{1,0:T(2,128)(2,1)} fusion(f32[1,8192]{1,0:T(1,128)S(1)} %bitcast.29, bf16[1,8192]{1,0:T(2,128)(2,1)S(1)} %copy-done.7), kind=kLoop, calls=%fused_computation.1 | loop fusion | flops 24576 | bytes 65536 | tf_op jit(solution)/shard_map/convert_element_type | solution.py:256
  (7 shorter events, 0.0 us)
Async XLA Ops:
  0.0 0.8 %copy-start.6 = (bf16[1,8192]{1,0:T(2,128)(2,1)S(1)}, bf16[1,8192]{1,0:T(2,128)(2,1)}, u32[]{:S(2)}) copy-start(bf16[1,8192]{1,0:T(2,128)(2,1)} %hidden_ref.1) | copy-start | bytes 49156
  0.8 0.8 %copy-start.8 = (f32[8192]{0:T(1024)S(1)}, f32[8192]{0:T(1024)}, u32[]{:S(2)}) copy-start(f32[8192]{0:T(1024)} %param.12) | copy-start | bytes 98308
  1.5 33.5 %copy-start.9 = (f32[1,16,8]{1,2,0:T(8,128)S(1)}, f32[1,16,8]{1,2,0:T(8,128)}, u32[]{:S(2)}) copy-start(f32[1,16,8]{1,2,0:T(8,128)} %param.19) | copy-start | bytes 1540
  1.5 33.5 %copy-start.10 = (f32[1,16,8]{1,2,0:T(8,128)S(1)}, f32[1,16,8]{1,2,0:T(8,128)}, u32[]{:S(2)}) copy-start(f32[1,16,8]{1,2,0:T(8,128)} %param.20) | copy-start | bytes 1540
  2.3 15.5 %all-to-all-start = ((bf16[32,16,128]{2,1,0:T(8,128)(2,1)}), bf16[32,16,128]{2,1,0:T(8,128)(2,1)S(1)}, u32[]{:S(2)}, u32[]{:S(2)}) async-start(bf16[32,16,128]{2,1,0:T(8,128)(2,1)} %shard_map.109), calls=%async_computation | async-start | bytes 262144 | tf_op jit(solution)/shard_map/all_to_all | solution.py:27
  17.9 2.2 %copy-start = (bf16[2048,1024]{1,0:T(8,128)(2,1)S(1)}, bf16[2048,1024]{1,0:T(8,128)(2,1)}, u32[]{:S(2)}) copy-start(bf16[2048,1024]{1,0:T(8,128)(2,1)} %w_query_ref.1) | copy-start | bytes 12582916
  20.1 1.0 %copy-start.4 = (bf16[2048,128]{1,0:T(8,128)(2,1)S(1)}, bf16[2048,128]{1,0:T(8,128)(2,1)}, u32[]{:S(2)}) copy-start(bf16[2048,128]{1,0:T(8,128)(2,1)} %key_ref.1) | copy-start | bytes 1572868
  21.1 1.0 %copy-start.5 = (bf16[2048,128]{1,0:T(8,128)(2,1)S(1)}, bf16[2048,128]{1,0:T(8,128)(2,1)}, u32[]{:S(2)}) copy-start(bf16[2048,128]{1,0:T(8,128)(2,1)} %value_ref.1) | copy-start | bytes 1572868
  23.8 11.2 %all-to-all-start.1 = ((f32[32,10,1,128]{3,2,1,0:T(1,128)}), f32[32,10,1,128]{3,2,1,0:T(1,128)S(1)}, u32[]{:S(2)}, u32[]{:S(2)}) async-start(f32[32,10,1,128]{3,2,1,0:T(1,128)} %bitcast.8), calls=%async_computation.1 | async-start | bytes 327680 | tf_op jit(solution)/shard_map/all_to_all | solution.py:27
  35.0 2.2 %copy-start.1 = (bf16[1,2048,1024]{2,1,0:T(8,128)(2,1)S(1)}, bf16[1,2048,1024]{2,1,0:T(8,128)(2,1)}, u32[]{:S(2)}) copy-start(bf16[1,2048,1024]{2,1,0:T(8,128)(2,1)} %param.17) | copy-start | bytes 12582916
  37.2 2.2 %copy-start.2 = (bf16[1,2048,1024]{2,1,0:T(8,128)(2,1)S(1)}, bf16[1,2048,1024]{2,1,0:T(8,128)(2,1)}, u32[]{:S(2)}) copy-start(bf16[1,2048,1024]{2,1,0:T(8,128)(2,1)} %param.18) | copy-start | bytes 12582916
  39.4 13.3 %copy-start.3 = (bf16[2048,1024]{1,0:T(8,128)(2,1)S(1)}, bf16[2048,1024]{1,0:T(8,128)(2,1)}, u32[]{:S(2)}) copy-start(bf16[2048,1024]{1,0:T(8,128)(2,1)} %weight_ref.1) | copy-start | bytes 12582916
  42.3 21.2 %copy-start.7 = (bf16[1,8192]{1,0:T(2,128)(2,1)S(1)}, bf16[1,8192]{1,0:T(2,128)(2,1)}, u32[]{:S(2)}) copy-start(bf16[1,8192]{1,0:T(2,128)(2,1)} %hidden_ref.1) | copy-start | bytes 49156

commit v3 on v2

v3 whole, which is shorter than its diff:
```python
import functools
import math

import jax
import jax.numpy as jnp
import numpy as np
from jax import lax
from jax.experimental import pallas as pl
from jax.experimental.pallas import tpu as pltpu
from jax.sharding import PartitionSpec as P

HQ = 64
KEY_VALUE_HEADS = 8
HEAD_SIZE = 128
GROUP = HQ // KEY_VALUE_HEADS

ROPE_BASE = 500000.0
NORM_EPS = 1e-05
MASKED_SCORE = -1e30

LANES = 128
VMEM = pl.BlockSpec(memory_space=pltpu.VMEM)
ANY = pl.BlockSpec(memory_space=pl.ANY)
PARAMS = pltpu.CompilerParams(vmem_limit_bytes=4 * 1024 * 1024)
COST = pl.CostEstimate(flops=20_000_000_000, transcendentals=0, bytes_accessed=0)


def exchange(blocks):
    return lax.all_to_all(blocks, ("gx", "gy"), split_axis=0, concat_axis=0, tiled=True)


def in_vmem(array):
    return pltpu.with_memory_space_constraint(array, pltpu.VMEM)


def in_hbm(array):
    return pltpu.with_memory_space_constraint(array, pltpu.HBM)


def norm_kernel(
    row_groups,
    length_hbm,
    freqs_hbm,
    hidden_hbm,
    gain_hbm,
    blocks_ref,
    turn_ref,
    length_ref,
    freqs_ref,
    hidden_ref,
    gain_ref,
    wide_ref,
    sems,
):
    pairs = (
        (length_hbm, length_ref),
        (freqs_hbm, freqs_ref),
        (hidden_hbm, hidden_ref),
        (gain_hbm, gain_ref),
    )
    copies = [pltpu.make_async_copy(*pair, sems.at[n]) for n, pair in enumerate(pairs)]
    for copy in copies:
        copy.start()
    for copy in copies[:2]:
        copy.wait()
    length = length_ref[...].astype(jnp.float32)
    angles = length * freqs_ref[0:1, :]
    turn_ref[0:1, :] = jnp.cos(angles)
    turn_ref[1:2, :] = jnp.sin(angles) * freqs_ref[1:2, :]
    turn_ref[2:3, :] = jnp.broadcast_to(length, (1, HEAD_SIZE))
    for copy in copies[2:]:
        copy.wait()
    rows = wide_ref.shape[0]
    for row in range(rows):
        wide_ref[row : row + 1, :] = hidden_ref[:, row * LANES : (row + 1) * LANES].astype(
            jnp.float32
        )
    wide = wide_ref[...]
    variance = jnp.sum(wide * wide, keepdims=True) * (1.0 / (rows * LANES))
    normed = (wide * lax.rsqrt(variance + NORM_EPS) * gain_ref[...]).astype(jnp.bfloat16)
    spread_blocks(normed, row_groups, blocks_ref)


def spread_blocks(rows, row_groups, blocks_ref):
    per_block = rows.shape[0] // row_groups
    column_groups = blocks_ref.shape[0] // row_groups
    for i in range(row_groups):
        part = rows[i * per_block : (i + 1) * per_block]
        for j in range(column_groups):
            blocks_ref[i * column_groups + j] = part


def flat_rows(blocks_ref):
    return jnp.concatenate([blocks_ref[:, k, :] for k in range(blocks_ref.shape[1])], axis=1)


def send_rows(products, out_ref):
    requests = products[0].shape[0]
    count = out_ref.shape[0] // requests
    parts = [
        product[:, start : start + LANES]
        for product in products
        for start in range(0, product.shape[1], LANES)
    ]
    for n, part in enumerate(parts):
        out_ref[pl.ds(n, requests, stride=count), :] = part


def project_kernel(blocks_ref, w_query_ref, key_ref, value_ref, out_ref):
    rows = flat_rows(blocks_ref)
    products = [
        jnp.dot(rows, ref[...], preferred_element_type=jnp.float32)
        for ref in (w_query_ref, key_ref, value_ref)
    ]
    if products[1].shape[1] % LANES:
        products[1:] = [jnp.concatenate(products[1:], axis=1)]
    send_rows(products, out_ref)


def output_kernel(blocks_ref, weight_ref, out_ref, wide_ref):
    rows = flat_rows(blocks_ref)
    send_rows([jnp.dot(rows, weight_ref[...], preferred_element_type=jnp.float32)], wide_ref)
    out_ref[...] = wide_ref[...].astype(out_ref.dtype)


def attend_kernel(
    row_groups,
    turn_ref,
    key_scale_ref,
    value_scale_ref,
    sums_ref,
    keys_ref,
    values_ref,
    blocks_ref,
    result_ref,
    factor_ref,
):
    capacity = keys_ref.shape[0]
    scale_blocks = key_scale_ref.shape[1]
    block = capacity // scale_blocks
    inv_root = 1.0 / math.sqrt(HEAD_SIZE)
    per_group = GROUP + 2
    cosine, sine = turn_ref[0:1, :], turn_ref[1:2, :]
    length = turn_ref[2:3, 0:1].astype(jnp.int32)
    spans = [slice(b * block, (b + 1) * block) for b in range(scale_blocks)]

    def rotate(wide):
        return (wide * cosine + pltpu.roll(wide, HEAD_SIZE // 2, 1) * sine).astype(jnp.bfloat16)

    def summed(first, count):
        total = sums_ref[first : first + count, :]
        for i in range(1, row_groups):
            start = i * KEY_VALUE_HEADS * per_group + first
            total = total + sums_ref[start : start + count, :]
        return total.astype(jnp.bfloat16).astype(jnp.float32)

    shape = (KEY_VALUE_HEADS, block)
    for b, span in enumerate(spans):
        factor_ref[0:KEY_VALUE_HEADS, span] = jnp.broadcast_to(
            key_scale_ref[:, b : b + 1] * inv_root, shape
        )
        factor_ref[KEY_VALUE_HEADS:, span] = jnp.broadcast_to(value_scale_ref[:, b : b + 1], shape)

    def factors(row, span):
        return jnp.broadcast_to(factor_ref[row : row + 1, span], (GROUP, block))

    positions = lax.broadcasted_iota(jnp.int32, (GROUP, block), 1)

    def score(g):
        query = rotate(summed(g * per_group, GROUP))
        new_key = rotate(summed(g * per_group + GROUP, 1))
        own = (
            jnp.sum(
                query.astype(jnp.float32) * new_key.astype(jnp.float32), axis=1, keepdims=True
            )
            * inv_root
        )
        raw = lax.dot_general(
            query,
            keys_ref[:, g * HEAD_SIZE : (g + 1) * HEAD_SIZE],
            (((1,), (1,)), ((), ())),
            preferred_element_type=jnp.float32,
        )
        return raw, own

    def weigh(g, raw, own):
        scores = [
            jnp.where(
                positions < length - b * block, raw[:, span] * factors(g, span), MASKED_SCORE
            )
            for b, span in enumerate(spans)
        ]
        peak = jnp.maximum(
            jnp.max(functools.reduce(jnp.maximum, scores), axis=1, keepdims=True), own
        )
        probs = [jnp.exp(part - peak) for part in scores]
        own_prob = jnp.exp(own - peak)
        total = jnp.sum(functools.reduce(jnp.add, probs), axis=1, keepdims=True) + own_prob
        weighted = [
            prob * factors(KEY_VALUE_HEADS + g, span) for prob, span in zip(probs, spans)
        ]
        new_value = summed(g * per_group + GROUP + 1, 1)
        own_part = own_prob.astype(jnp.bfloat16).astype(jnp.float32) * new_value
        return weighted, own_part, total

    def finish(g, weighed):
        lhs = jnp.concatenate(
            [jnp.concatenate(parts, axis=0) for parts in zip(weighed[0][0], weighed[1][0])], axis=1
        )
        both = jnp.dot(
            lhs.astype(jnp.bfloat16),
            values_ref[:, g * HEAD_SIZE : (g + 2) * HEAD_SIZE],
            preferred_element_type=jnp.float32,
        )
        for n, (_, own_part, total) in enumerate(weighed):
            part = both[n * GROUP : (n + 1) * GROUP, n * HEAD_SIZE : (n + 1) * HEAD_SIZE]
            result_ref[(g + n) * GROUP : (g + n + 1) * GROUP, :] = (part + own_part) / total

    ahead = [score(0), score(1)]
    for g in range(0, KEY_VALUE_HEADS, 2):
        now = ahead
        if g + 2 < KEY_VALUE_HEADS:
            ahead = [score(g + 2), score(g + 3)]
        finish(g, [weigh(g + n, *now[n]) for n in range(2)])
    spread_blocks(result_ref[...].astype(jnp.bfloat16), row_groups, blocks_ref)


def rotation_rows():
    half = HEAD_SIZE // 2
    freqs = ROPE_BASE ** (-(np.arange(half) * 2.0) / HEAD_SIZE)
    signs = np.concatenate([-np.ones(half), np.ones(half)])
    return jnp.asarray(np.stack([np.tile(freqs, 2), signs]), jnp.float32)


def body(
    hidden_in,
    norm_gain,
    w_query,
    key_weight,
    value_weight,
    w_output,
    key_cache_units,
    value_cache_units,
    key_scale,
    value_block_scale,
    lengths,
):
    row_groups, column_groups = lax.axis_size("gx"), lax.axis_size("gy")
    devices = row_groups * column_groups
    width = hidden_in.shape[1]
    slice_rows = width // row_groups // LANES
    query_cols, key_cols = w_query.shape[1], key_weight.shape[1]
    out_cols = w_output.shape[1]
    blocks_type = jax.ShapeDtypeStruct((devices, slice_rows, LANES), jnp.bfloat16)

    blocks, turn = pl.pallas_call(
        functools.partial(norm_kernel, row_groups),
        out_shape=[blocks_type, jax.ShapeDtypeStruct((8, HEAD_SIZE), jnp.float32)],
        in_specs=[ANY] * 4,
        out_specs=[VMEM, VMEM],
        scratch_shapes=[
            pltpu.VMEM((1, 1), jnp.int32),
            pltpu.VMEM((2, HEAD_SIZE), jnp.float32),
            pltpu.VMEM((1, width), hidden_in.dtype),
            pltpu.VMEM((width // LANES, LANES), jnp.float32),
            pltpu.VMEM((width // LANES, LANES), jnp.float32),
            pltpu.SemaphoreType.DMA((4,)),
        ],
        compiler_params=PARAMS,
        cost_estimate=COST,
    )(
        lengths.reshape(1, 1),
        in_hbm(rotation_rows()),
        in_hbm(hidden_in),
        in_hbm(norm_gain.reshape(-1, LANES)),
    )

    sent_rows = (query_cols + 2 * key_cols) // LANES
    partial = pl.pallas_call(
        project_kernel,
        out_shape=jax.ShapeDtypeStruct((devices * sent_rows, LANES), jnp.float32),
        in_specs=[VMEM] * 4,
        out_specs=VMEM,
        compiler_params=PARAMS,
        cost_estimate=COST,
    )(exchange(blocks), in_vmem(w_query), in_vmem(key_weight), in_vmem(value_weight))
    sums = exchange(partial.reshape(devices, sent_rows, 1, LANES))
    if key_cols != HEAD_SIZE:
        sums = sums.reshape(row_groups, column_groups, sent_rows * LANES)
        sums = jnp.concatenate(
            [
                part.reshape(row_groups, KEY_VALUE_HEADS, -1, HEAD_SIZE)
                for part in jnp.split(sums, (query_cols, query_cols + key_cols), axis=2)
            ],
            axis=2,
        )
    sums = sums.reshape(-1, LANES)

    attended = pl.pallas_call(
        functools.partial(attend_kernel, row_groups),
        out_shape=blocks_type,
        in_specs=[VMEM] * 6,
        out_specs=VMEM,
        scratch_shapes=[
            pltpu.VMEM((HQ, HEAD_SIZE), jnp.float32),
            pltpu.VMEM((2 * KEY_VALUE_HEADS, key_cache_units.shape[1]), jnp.float32),
        ],
        compiler_params=PARAMS,
        cost_estimate=COST,
    )(
        turn,
        key_scale[0].T,
        value_block_scale[0].T,
        sums,
        in_vmem(key_cache_units[0]),
        in_vmem(value_cache_units[0]),
    )

    out_rows = out_cols // LANES
    partial = pl.pallas_call(
        output_kernel,
        out_shape=jax.ShapeDtypeStruct((devices * out_rows, LANES), jnp.bfloat16),
        in_specs=[VMEM] * 2,
        out_specs=VMEM,
        scratch_shapes=[pltpu.VMEM((devices * out_rows, LANES), jnp.float32)],
        compiler_params=PARAMS,
        cost_estimate=COST,
    )(exchange(attended), in_vmem(w_output))
    update = exchange(partial.reshape(devices, out_rows, LANES)).astype(jnp.float32)
    update = jnp.sum(update.reshape(row_groups, column_groups * out_rows, LANES), axis=0)
    return (hidden_in.astype(jnp.float32) + update.reshape(1, width)).astype(jnp.bfloat16)


def solution(mesh):
    placed = (
        P(("gx", "gy"), None),
        P(),
        P("gx", "gy"),
        P("gx", "gy"),
        P("gx", "gy"),
        P("gx", "gy"),
        P(("gx", "gy"), None, None),
        P(("gx", "gy"), None, None),
        P(("gx", "gy"), None, None),
        P(("gx", "gy"), None, None),
        P(("gx", "gy")),
    )
    return jax.shard_map(
        body, mesh=mesh, in_specs=placed, out_specs=P(("gx", "gy"), None), check_vma=False
    )
```

time: 64.8 us -> 51.9 us (0.80)
  blocking collectives: 20.3 us -> 45.3 us
  waiting for transfers between devices: 15.9 us -> 0 us
  local copies, waits for them, and re-layouts: 10.2 us -> 0.05 us
  starting transfers between devices: 9.87 us -> 0 us
  Pallas kernels: 6.33 us -> 4.9 us
    all_to_all x2 -> x4, blocking collectives: 20.3 us -> 45.3 us  [exchange(): lax.all_to_all(blocks, ('gx', 'gy'), split_axis=0, concat_axis=0, tiled=T...]
    all_to_all x2 -> x0, waiting for transfers between devices: 15.9 us -> none  [exchange(): lax.all_to_all(blocks, ('gx', 'gy'), split_axis=0, concat_axis=0, tiled=T...]
    unnamed x22 -> x18, local copies, waits for them, and re-layouts: 10.2 us -> 0.05 us
    all_to_all x2 -> x0, starting transfers between devices: 9.87 us -> none  [exchange(): lax.all_to_all(blocks, ('gx', 'gy'), split_axis=0, concat_axis=0, tiled=T...]
    pallas_call x1, Pallas kernels: 2.98 us -> 1.89 us  [body(): pl.pallas_call(functools.partial(attend_kernel, row_groups), out_shape=bl...]
    pallas_call x1, Pallas kernels: 1.67 us -> 0.99 us  [body(): pl.pallas_call(project_kernel, out_shape=jax.ShapeDtypeStruct((devices *...]
  transfers between devices with their start and end apart: 2 -> 0, of which waited for: 2 -> 0; matrix products, arithmetic and copies ran while one was open for 0% -> 0% of each run, Pallas kernels for 0% -> 0%
where the time goes in v3:
time: 51.9 us; the launch traced here: 51.7 us
  blocking collectives  45.3 us (87%)
  Pallas kernels  4.9 us (9%)
  between operations  0.77 us (1%)
  other arithmetic  0.67 us (1%)
    all_to_all x4, blocking collectives, exchange(): lax.all_to_all(blocks, ('gx', 'gy'), split_axis=0, concat_axis=0, tiled=T...  45.3 us
    pallas_call x1, Pallas kernels, body(): pl.pallas_call(functools.partial(attend_kernel, row_groups), out_shape=bl...  1.89 us
    pallas_call x1, Pallas kernels, body(): pl.pallas_call(functools.partial(norm_kernel, row_groups), out_shape=[blo...  1.16 us

profile of v3, /device:TPU:0, one launch (start us, length us, event | category | flops | bytes accessed | tf_op | source)
XLA Modules:
  0.0 51.7 jit_solution(476100489527845361)
XLA Ops:
  0.7 0.0 copy-start
  0.7 0.0 copy-start.4
  0.7 0.0 copy-start.5
  0.7 1.2 %shard_map.118 = (bf16[32,16,128]{2,1,0:T(8,128)(2,1)S(1)}, f32[8,128]{1,0:T(8,128)S(1)}) custom-call(s32[1,1]{1,0:T(1,128)} %bitcast.18.length_hbm, f32[2,128]{1,0:T(2,128)} %constant.4.clone.freqs_hbm, bf16[1,8192]{1,0:T(2,128)(2,1)} %hidden_hbm.1, f32[64,128]{1,0:T(8,128)} %bitcast.28), custom_call_target="tpu_custom_call" | custom-call | flops 20000000000 | tf_op jit(solution)/shard_map/pallas_call | solution.py:256
  1.8 15.3 %all_to_all.20.blocks_ref = bf16[32,16,128]{2,1,0:T(8,128)(2,1)S(1)} all-to-all(bf16[32,16,128]{2,1,0:T(8,128)(2,1)S(1)} %get-tuple-element.8), channel_id=1, replica_groups=mesh['gx'=4,'gy'=8] {'gx','gy'}, dimensions={0} | all-to-all | bytes 262144 | tf_op jit(solution)/shard_map/all_to_all | solution.py:29
  17.2 0.0 copy-done
  17.2 0.0 copy-done.4
  17.2 0.0 copy-done.5
  17.2 0.0 copy-start.1
  17.2 0.0 copy-start.2
  17.2 0.0 copy-start.6
  17.2 0.0 copy-start.7
  17.2 1.0 %shard_map.119 = f32[320,128]{1,0:T(8,128)S(1)} custom-call(bf16[32,16,128]{2,1,0:T(8,128)(2,1)S(1)} %all_to_all.20.blocks_ref, bf16[2048,1024]{1,0:T(8,128)(2,1)S(1)} %copy-done, bf16[2048,128]{1,0:T(8,128)(2,1)S(1)} %copy-done.4, bf16[2048,128]{1,0:T(8,128)(2,1)S(1)} %copy-done.5), custom_call_target="tpu_custom_call" | custom-call | flops 20000000000 | tf_op jit(solution)/shard_map/pallas_call | solution.py:279
  18.2 10.5 %all_to_all.21 = f32[32,10,1,128]{3,2,1,0:T(1,128)S(1)} all-to-all(f32[32,10,1,128]{3,2,1,0:T(1,128)S(1)} %bitcast.20), channel_id=1, replica_groups=mesh['gx'=4,'gy'=8] {'gx','gy'}, dimensions={0} | all-to-all | bytes 327680 | tf_op jit(solution)/shard_map/all_to_all | solution.py:29
  28.8 0.0 copy-done.1
  28.8 0.0 copy-done.2
  28.8 0.0 copy-done.6
  28.8 0.0 copy-done.7
  28.8 0.0 copy-start.3
  28.8 1.9 %shard_map.120 = bf16[32,16,128]{2,1,0:T(8,128)(2,1)S(1)} custom-call(f32[8,128]{1,0:T(8,128)S(1)} %get-tuple-element.7.turn_ref, f32[8,16]{1,0:T(8,128)S(1)} %bitcast.24, f32[8,16]{1,0:T(8,128)S(1)} %bitcast.25, f32[320,128]{1,0:T(8,128)S(1)} %bitcast.19, bf16[2048,1024]{1,0:T(8,128)(2,1)S(1)} %bitcast.22, bf16[2048,1024]{1,0:T(8,128)(2,1)S(1)} %bitcast.23), custom_call_target="tpu_custom_call" | custom-call | flops 20000000000 | tf_op jit(solution)/shard_map/pallas_call | solution.py:299
  30.7 10.3 %all_to_all.22.blocks_ref = bf16[32,16,128]{2,1,0:T(8,128)(2,1)S(1)} all-to-all(bf16[32,16,128]{2,1,0:T(8,128)(2,1)S(1)} %shard_map.120), channel_id=1, replica_groups=mesh['gx'=4,'gy'=8] {'gx','gy'}, dimensions={0} | all-to-all | bytes 262144 | tf_op jit(solution)/shard_map/all_to_all | solution.py:29
  41.0 0.0 copy-done.3
  41.0 0.0 copy-start.8
  41.0 0.9 %shard_map.121 = bf16[256,128]{1,0:T(8,128)(2,1)S(1)} custom-call(bf16[32,16,128]{2,1,0:T(8,128)(2,1)S(1)} %all_to_all.22.blocks_ref, bf16[2048,1024]{1,0:T(8,128)(2,1)S(1)} %copy-done.3), custom_call_target="tpu_custom_call" | custom-call | flops 20000000000 | tf_op jit(solution)/shard_map/pallas_call | solution.py:320
  41.8 9.2 %all_to_all.23 = bf16[32,8,128]{2,1,0:T(8,128)(2,1)S(1)} all-to-all(bf16[32,8,128]{2,1,0:T(8,128)(2,1)S(1)} %bitcast.21), channel_id=1, replica_groups=mesh['gx'=4,'gy'=8] {'gx','gy'}, dimensions={0} | all-to-all | bytes 131072 | tf_op jit(solution)/shard_map/all_to_all | solution.py:29
  51.0 0.0 copy-done.8
  51.0 0.7 %add_convert_fusion = bf16[1,8192]{1,0:T(2,128)(2,1)} fusion(f32[1,8192]{1,0:T(1,128)S(1)} %bitcast.27, bf16[1,8192]{1,0:T(2,128)(2,1)S(1)} %copy-done.8), kind=kLoop, calls=%fused_computation.1 | loop fusion | flops 24576 | bytes 65536 | tf_op jit(solution)/shard_map/convert_element_type | solution.py:331
  (1 shorter events, 0.0 us)
Async XLA Ops:
  0.7 16.5 %copy-start = (bf16[2048,1024]{1,0:T(8,128)(2,1)S(1)}, bf16[2048,1024]{1,0:T(8,128)(2,1)}, u32[]{:S(2)}) copy-start(bf16[2048,1024]{1,0:T(8,128)(2,1)} %w_query_ref.1) | copy-start | bytes 12582916
  0.7 16.5 %copy-start.4 = (bf16[2048,128]{1,0:T(8,128)(2,1)S(1)}, bf16[2048,128]{1,0:T(8,128)(2,1)}, u32[]{:S(2)}) copy-start(bf16[2048,128]{1,0:T(8,128)(2,1)} %key_ref.1) | copy-start | bytes 1572868
  0.7 16.5 %copy-start.5 = (bf16[2048,128]{1,0:T(8,128)(2,1)S(1)}, bf16[2048,128]{1,0:T(8,128)(2,1)}, u32[]{:S(2)}) copy-start(bf16[2048,128]{1,0:T(8,128)(2,1)} %value_ref.1) | copy-start | bytes 1572868
  17.2 11.6 %copy-start.1 = (bf16[1,2048,1024]{2,1,0:T(8,128)(2,1)S(1)}, bf16[1,2048,1024]{2,1,0:T(8,128)(2,1)}, u32[]{:S(2)}) copy-start(bf16[1,2048,1024]{2,1,0:T(8,128)(2,1)} %param.18) | copy-start | bytes 12582916
  17.2 11.6 %copy-start.2 = (bf16[1,2048,1024]{2,1,0:T(8,128)(2,1)S(1)}, bf16[1,2048,1024]{2,1,0:T(8,128)(2,1)}, u32[]{:S(2)}) copy-start(bf16[1,2048,1024]{2,1,0:T(8,128)(2,1)} %param.19) | copy-start | bytes 12582916
  17.2 11.6 %copy-start.6 = (f32[1,16,8]{1,2,0:T(8,128)S(1)}, f32[1,16,8]{1,2,0:T(8,128)}, u32[]{:S(2)}) copy-start(f32[1,16,8]{1,2,0:T(8,128)} %param.20) | copy-start | bytes 1540
  17.2 11.6 %copy-start.7 = (f32[1,16,8]{1,2,0:T(8,128)S(1)}, f32[1,16,8]{1,2,0:T(8,128)}, u32[]{:S(2)}) copy-start(f32[1,16,8]{1,2,0:T(8,128)} %param.21) | copy-start | bytes 1540
  28.8 12.2 %copy-start.3 = (bf16[2048,1024]{1,0:T(8,128)(2,1)S(1)}, bf16[2048,1024]{1,0:T(8,128)(2,1)}, u32[]{:S(2)}) copy-start(bf16[2048,1024]{1,0:T(8,128)(2,1)} %weight_ref.1) | copy-start | bytes 12582916
  41.0 10.1 %copy-start.8 = (bf16[1,8192]{1,0:T(2,128)(2,1)S(1)}, bf16[1,8192]{1,0:T(2,128)(2,1)}, u32[]{:S(2)}) copy-start(bf16[1,8192]{1,0:T(2,128)(2,1)} %hidden_hbm.1) | copy-start | bytes 49156

commit v4 on v3

--- a/solution.py
+++ b/solution.py
@@ -3,7 +3,6 @@
 
 import jax
 import jax.numpy as jnp
-import numpy as np
 from jax import lax
 from jax.experimental import pallas as pl
 from jax.experimental.pallas import tpu as pltpu
@@ -20,7 +19,7 @@
 
 LANES = 128
 VMEM = pl.BlockSpec(memory_space=pltpu.VMEM)
-ANY = pl.BlockSpec(memory_space=pl.ANY)
+SMEM = pl.BlockSpec(memory_space=pltpu.SMEM)
 PARAMS = pltpu.CompilerParams(vmem_limit_bytes=4 * 1024 * 1024)
 COST = pl.CostEstimate(flops=20_000_000_000, transcendentals=0, bytes_accessed=0)
 
@@ -33,43 +32,26 @@
     return pltpu.with_memory_space_constraint(array, pltpu.VMEM)
 
 
-def in_hbm(array):
-    return pltpu.with_memory_space_constraint(array, pltpu.HBM)
-
-
-def norm_kernel(
-    row_groups,
-    length_hbm,
-    freqs_hbm,
-    hidden_hbm,
-    gain_hbm,
-    blocks_ref,
-    turn_ref,
-    length_ref,
-    freqs_ref,
-    hidden_ref,
-    gain_ref,
-    wide_ref,
-    sems,
-):
-    pairs = (
-        (length_hbm, length_ref),
-        (freqs_hbm, freqs_ref),
-        (hidden_hbm, hidden_ref),
-        (gain_hbm, gain_ref),
-    )
-    copies = [pltpu.make_async_copy(*pair, sems.at[n]) for n, pair in enumerate(pairs)]
-    for copy in copies:
-        copy.start()
-    for copy in copies[:2]:
-        copy.wait()
-    length = length_ref[...].astype(jnp.float32)
-    angles = length * freqs_ref[0:1, :]
+def freqs_kernel(table_ref):
+    half = HEAD_SIZE // 2
+    lanes = lax.broadcasted_iota(jnp.int32, (1, HEAD_SIZE), 1)
+    places = jnp.where(lanes < half, lanes, lanes - half)
+    freqs = jnp.zeros((1, HEAD_SIZE), jnp.float32)
+    for i in range(half):
+        freqs = jnp.where(places == i, ROPE_BASE ** (-2.0 * i / HEAD_SIZE), freqs)
+    table_ref[0:1, :] = freqs
+    table_ref[1:2, :] = jnp.where(lanes < half, -1.0, 1.0)
+
+
+def turn_kernel(length_ref, table_ref, turn_ref):
+    length = length_ref[0].astype(jnp.float32)
+    angles = length * table_ref[0:1, :]
     turn_ref[0:1, :] = jnp.cos(angles)
-    turn_ref[1:2, :] = jnp.sin(angles) * freqs_ref[1:2, :]
-    turn_ref[2:3, :] = jnp.broadcast_to(length, (1, HEAD_SIZE))
-    for copy in copies[2:]:
-        copy.wait()
+    turn_ref[1:2, :] = jnp.sin(angles) * table_ref[1:2, :]
+    turn_ref[2:3, :] = jnp.full((1, HEAD_SIZE), length)
+
+
+def norm_kernel(row_groups, turn_ref, hidden_ref, gain_ref, blocks_ref, wide_ref):
     rows = wide_ref.shape[0]
     for row in range(rows):
         wide_ref[row : row + 1, :] = hidden_ref[:, row * LANES : (row + 1) * LANES].astype(
@@ -225,13 +207,6 @@
     spread_blocks(result_ref[...].astype(jnp.bfloat16), row_groups, blocks_ref)
 
 
-def rotation_rows():
-    half = HEAD_SIZE // 2
-    freqs = ROPE_BASE ** (-(np.arange(half) * 2.0) / HEAD_SIZE)
-    signs = np.concatenate([-np.ones(half), np.ones(half)])
-    return jnp.asarray(np.stack([np.tile(freqs, 2), signs]), jnp.float32)
-
-
 def body(
     hidden_in,
     norm_gain,
@@ -253,27 +228,31 @@
     out_cols = w_output.shape[1]
     blocks_type = jax.ShapeDtypeStruct((devices, slice_rows, LANES), jnp.bfloat16)
 
-    blocks, turn = pl.pallas_call(
+    turn_type = jax.ShapeDtypeStruct((8, HEAD_SIZE), jnp.float32)
+    table = pl.pallas_call(
+        freqs_kernel,
+        out_shape=turn_type,
+        out_specs=VMEM,
+        compiler_params=PARAMS,
+        cost_estimate=COST,
+    )()
+    lengths, table = lax.optimization_barrier((lengths, table))
+    turn = pl.pallas_call(
+        turn_kernel,
+        out_shape=turn_type,
+        in_specs=[SMEM, VMEM],
+        out_specs=VMEM,
+        compiler_params=PARAMS,
+    )(lengths, table)
+    blocks = pl.pallas_call(
         functools.partial(norm_kernel, row_groups),
-        out_shape=[blocks_type, jax.ShapeDtypeStruct((8, HEAD_SIZE), jnp.float32)],
-        in_specs=[ANY] * 4,
-        out_specs=[VMEM, VMEM],
-        scratch_shapes=[
-            pltpu.VMEM((1, 1), jnp.int32),
-            pltpu.VMEM((2, HEAD_SIZE), jnp.float32),
-            pltpu.VMEM((1, width), hidden_in.dtype),
-            pltpu.VMEM((width // LANES, LANES), jnp.float32),
-            pltpu.VMEM((width // LANES, LANES), jnp.float32),
-            pltpu.SemaphoreType.DMA((4,)),
-        ],
-        compiler_params=PARAMS,
-        cost_estimate=COST,
-    )(
-        lengths.reshape(1, 1),
-        in_hbm(rotation_rows()),
-        in_hbm(hidden_in),
-        in_hbm(norm_gain.reshape(-1, LANES)),
-    )
+        out_shape=blocks_type,
+        in_specs=[VMEM] * 3,
+        out_specs=VMEM,
+        scratch_shapes=[pltpu.VMEM((width // LANES, LANES), jnp.float32)],
+        compiler_params=PARAMS,
+        cost_estimate=COST,
+    )(turn, in_vmem(hidden_in), in_vmem(norm_gain.reshape(-1, LANES)))
 
     sent_rows = (query_cols + 2 * key_cols) // LANES
     partial = pl.pallas_call(

time: 51.9 us -> 51 us (0.983)
  Pallas kernels: 4.9 us -> 3.98 us
    pallas_call x1 -> x3, Pallas kernels: 1.16 us -> 0.25 us  [the longest x1 0.16 us: body(): pl.pallas_call(functools.partial(norm_kernel, row_groups), out_shape=bloc...]
where the time goes in v4:
time: 51 us; the launch traced here: 50.8 us
  blocking collectives  45.3 us (89%)
  Pallas kernels  3.98 us (8%)
  between operations  0.75 us (1%)
  other arithmetic  0.67 us (1%)
    all_to_all x4, blocking collectives, exchange(): lax.all_to_all(blocks, ('gx', 'gy'), split_axis=0, concat_axis=0, tiled=T...  45.3 us
    pallas_call x1, Pallas kernels, body(): pl.pallas_call(functools.partial(attend_kernel, row_groups), out_shape=bl...  1.89 us

profile of v4, /device:TPU:0, one launch (start us, length us, event | category | flops | bytes accessed | tf_op | source)
XLA Modules:
  0.0 50.8 jit_solution(8697238923018233436)
XLA Ops:
  0.0 0.0 copy-start
  0.0 0.0 copy-start.7
  0.7 0.0 copy-done
  0.8 0.0 copy-done.7
  0.8 0.0 copy-start.1
  0.8 0.0 copy-start.5
  0.8 0.0 copy-start.6
  0.8 0.2 shard_map.111
  1.0 15.3 %all_to_all.20.blocks_ref = bf16[32,16,128]{2,1,0:T(8,128)(2,1)S(1)} all-to-all(bf16[32,16,128]{2,1,0:T(8,128)(2,1)S(1)} %shard_map.111), channel_id=1, replica_groups=mesh['gx'=4,'gy'=8] {'gx','gy'}, dimensions={0} | all-to-all | bytes 262144 | tf_op jit(solution)/shard_map/all_to_all | solution.py:28
  16.3 0.0 copy-done.1
  16.3 0.0 copy-done.5
  16.3 0.0 copy-done.6
  16.3 0.0 copy-start.2
  16.3 0.0 copy-start.3
  16.3 0.0 copy-start.8
  16.3 0.0 copy-start.9
  16.4 1.0 %shard_map.112 = f32[320,128]{1,0:T(8,128)S(1)} custom-call(bf16[32,16,128]{2,1,0:T(8,128)(2,1)S(1)} %all_to_all.20.blocks_ref, bf16[2048,1024]{1,0:T(8,128)(2,1)S(1)} %copy-done.1, bf16[2048,128]{1,0:T(8,128)(2,1)S(1)} %copy-done.5, bf16[2048,128]{1,0:T(8,128)(2,1)S(1)} %copy-done.6), custom_call_target="tpu_custom_call" | custom-call | flops 20000000000 | tf_op jit(solution)/shard_map/pallas_call | solution.py:258
  17.4 10.5 %all_to_all.21 = f32[32,10,1,128]{3,2,1,0:T(1,128)S(1)} all-to-all(f32[32,10,1,128]{3,2,1,0:T(1,128)S(1)} %bitcast.18), channel_id=1, replica_groups=mesh['gx'=4,'gy'=8] {'gx','gy'}, dimensions={0} | all-to-all | bytes 327680 | tf_op jit(solution)/shard_map/all_to_all | solution.py:28
  27.9 0.0 copy-done.2
  27.9 0.0 copy-done.3
  27.9 0.0 copy-done.8
  27.9 0.0 copy-done.9
  27.9 0.0 copy-start.4
  27.9 1.9 %shard_map.113 = bf16[32,16,128]{2,1,0:T(8,128)(2,1)S(1)} custom-call(f32[8,128]{1,0:T(8,128)S(1)} %shard_map.110.turn_ref, f32[8,16]{1,0:T(8,128)S(1)} %bitcast.23, f32[8,16]{1,0:T(8,128)S(1)} %bitcast.24, f32[320,128]{1,0:T(8,128)S(1)} %bitcast.17, bf16[2048,1024]{1,0:T(8,128)(2,1)S(1)} %bitcast.20, bf16[2048,1024]{1,0:T(8,128)(2,1)S(1)} %bitcast.21), custom_call_target="tpu_custom_call" | custom-call | flops 20000000000 | tf_op jit(solution)/shard_map/pallas_call | solution.py:278
  29.8 10.3 %all_to_all.22.blocks_ref = bf16[32,16,128]{2,1,0:T(8,128)(2,1)S(1)} all-to-all(bf16[32,16,128]{2,1,0:T(8,128)(2,1)S(1)} %shard_map.113), channel_id=1, replica_groups=mesh['gx'=4,'gy'=8] {'gx','gy'}, dimensions={0} | all-to-all | bytes 262144 | tf_op jit(solution)/shard_map/all_to_all | solution.py:28
  40.1 0.0 copy-done.4
  40.1 0.9 %shard_map.114 = bf16[256,128]{1,0:T(8,128)(2,1)S(1)} custom-call(bf16[32,16,128]{2,1,0:T(8,128)(2,1)S(1)} %all_to_all.22.blocks_ref, bf16[2048,1024]{1,0:T(8,128)(2,1)S(1)} %copy-done.4), custom_call_target="tpu_custom_call" | custom-call | flops 20000000000 | tf_op jit(solution)/shard_map/pallas_call | solution.py:299
  41.0 9.2 %all_to_all.23 = bf16[32,8,128]{2,1,0:T(8,128)(2,1)S(1)} all-to-all(bf16[32,8,128]{2,1,0:T(8,128)(2,1)S(1)} %bitcast.19), channel_id=1, replica_groups=mesh['gx'=4,'gy'=8] {'gx','gy'}, dimensions={0} | all-to-all | bytes 131072 | tf_op jit(solution)/shard_map/all_to_all | solution.py:28
  50.1 0.7 %add_convert_fusion = bf16[1,8192]{1,0:T(2,128)(2,1)} fusion(f32[1,8192]{1,0:T(1,128)S(1)} %bitcast.26, bf16[1,8192]{1,0:T(2,128)(2,1)S(1)} %copy-done), kind=kLoop, calls=%fused_computation.1 | loop fusion | flops 24576 | bytes 65536 | tf_op jit(solution)/shard_map/convert_element_type | solution.py:310
  (3 shorter events, 0.1 us)
Async XLA Ops:
  0.0 0.8 %copy-start = (bf16[1,8192]{1,0:T(2,128)(2,1)S(1)}, bf16[1,8192]{1,0:T(2,128)(2,1)}, u32[]{:S(2)}) copy-start(bf16[1,8192]{1,0:T(2,128)(2,1)} %hidden_ref.1) | copy-start | bytes 49156
  0.0 0.8 %copy-start.7 = (f32[8192]{0:T(1024)S(1)}, f32[8192]{0:T(1024)}, u32[]{:S(2)}) copy-start(f32[8192]{0:T(1024)} %param.12) | copy-start | bytes 98308
  0.8 15.5 %copy-start.1 = (bf16[2048,1024]{1,0:T(8,128)(2,1)S(1)}, bf16[2048,1024]{1,0:T(8,128)(2,1)}, u32[]{:S(2)}) copy-start(bf16[2048,1024]{1,0:T(8,128)(2,1)} %w_query_ref.1) | copy-start | bytes 12582916
  0.8 15.5 %copy-start.5 = (bf16[2048,128]{1,0:T(8,128)(2,1)S(1)}, bf16[2048,128]{1,0:T(8,128)(2,1)}, u32[]{:S(2)}) copy-start(bf16[2048,128]{1,0:T(8,128)(2,1)} %key_ref.1) | copy-start | bytes 1572868
  0.8 15.5 %copy-start.6 = (bf16[2048,128]{1,0:T(8,128)(2,1)S(1)}, bf16[2048,128]{1,0:T(8,128)(2,1)}, u32[]{:S(2)}) copy-start(bf16[2048,128]{1,0:T(8,128)(2,1)} %value_ref.1) | copy-start | bytes 1572868
  16.3 11.6 %copy-start.2 = (bf16[1,2048,1024]{2,1,0:T(8,128)(2,1)S(1)}, bf16[1,2048,1024]{2,1,0:T(8,128)(2,1)}, u32[]{:S(2)}) copy-start(bf16[1,2048,1024]{2,1,0:T(8,128)(2,1)} %param.17) | copy-start | bytes 12582916
  16.3 11.6 %copy-start.3 = (bf16[1,2048,1024]{2,1,0:T(8,128)(2,1)S(1)}, bf16[1,2048,1024]{2,1,0:T(8,128)(2,1)}, u32[]{:S(2)}) copy-start(bf16[1,2048,1024]{2,1,0:T(8,128)(2,1)} %param.18) | copy-start | bytes 12582916
  16.3 11.6 %copy-start.8 = (f32[1,16,8]{1,2,0:T(8,128)S(1)}, f32[1,16,8]{1,2,0:T(8,128)}, u32[]{:S(2)}) copy-start(f32[1,16,8]{1,2,0:T(8,128)} %param.19) | copy-start | bytes 1540
  16.3 11.6 %copy-start.9 = (f32[1,16,8]{1,2,0:T(8,128)S(1)}, f32[1,16,8]{1,2,0:T(8,128)}, u32[]{:S(2)}) copy-start(f32[1,16,8]{1,2,0:T(8,128)} %param.20) | copy-start | bytes 1540
  27.9 12.2 %copy-start.4 = (bf16[2048,1024]{1,0:T(8,128)(2,1)S(1)}, bf16[2048,1024]{1,0:T(8,128)(2,1)}, u32[]{:S(2)}) copy-start(bf16[2048,1024]{1,0:T(8,128)(2,1)} %weight_ref.1) | copy-start | bytes 12582916

commit v5 on v4

--- a/solution.py
+++ b/solution.py
@@ -21,11 +21,20 @@
 VMEM = pl.BlockSpec(memory_space=pltpu.VMEM)
 SMEM = pl.BlockSpec(memory_space=pltpu.SMEM)
 PARAMS = pltpu.CompilerParams(vmem_limit_bytes=4 * 1024 * 1024)
+SENT_SCALE = 16.0
 COST = pl.CostEstimate(flops=20_000_000_000, transcendentals=0, bytes_accessed=0)
 
 
 def exchange(blocks):
     return lax.all_to_all(blocks, ("gx", "gy"), split_axis=0, concat_axis=0, tiled=True)
+
+
+def exchange_sums(partial, devices):
+    sent = (partial * SENT_SCALE).astype(jnp.float16)
+    count = partial.shape[0] // devices
+    pair = 8 if count % 8 == 0 else 2 if count % 2 == 0 else 1
+    arrived = exchange(sent.reshape(devices, -1, pair, LANES)).reshape(partial.shape)
+    return arrived.astype(jnp.float32) * (1.0 / SENT_SCALE)
 
 
 def in_vmem(array):
@@ -99,10 +108,9 @@
     send_rows(products, out_ref)
 
 
-def output_kernel(blocks_ref, weight_ref, out_ref, wide_ref):
+def output_kernel(blocks_ref, weight_ref, out_ref):
     rows = flat_rows(blocks_ref)
-    send_rows([jnp.dot(rows, weight_ref[...], preferred_element_type=jnp.float32)], wide_ref)
-    out_ref[...] = wide_ref[...].astype(out_ref.dtype)
+    send_rows([jnp.dot(rows, weight_ref[...], preferred_element_type=jnp.float32)], out_ref)
 
 
 def attend_kernel(
@@ -263,7 +271,7 @@
         compiler_params=PARAMS,
         cost_estimate=COST,
     )(exchange(blocks), in_vmem(w_query), in_vmem(key_weight), in_vmem(value_weight))
-    sums = exchange(partial.reshape(devices, sent_rows, 1, LANES))
+    sums = exchange_sums(partial, devices)
     if key_cols != HEAD_SIZE:
         sums = sums.reshape(row_groups, column_groups, sent_rows * LANES)
         sums = jnp.concatenate(
@@ -298,14 +306,13 @@
     out_rows = out_cols // LANES
     partial = pl.pallas_call(
         output_kernel,
-        out_shape=jax.ShapeDtypeStruct((devices * out_rows, LANES), jnp.bfloat16),
+        out_shape=jax.ShapeDtypeStruct((devices * out_rows, LANES), jnp.float32),
         in_specs=[VMEM] * 2,
         out_specs=VMEM,
-        scratch_shapes=[pltpu.VMEM((devices * out_rows, LANES), jnp.float32)],
         compiler_params=PARAMS,
         cost_estimate=COST,
     )(exchange(attended), in_vmem(w_output))
-    update = exchange(partial.reshape(devices, out_rows, LANES)).astype(jnp.float32)
+    update = exchange_sums(partial, devices)
     update = jnp.sum(update.reshape(row_groups, column_groups * out_rows, LANES), axis=0)
     return (hidden_in.astype(jnp.float32) + update.reshape(1, width)).astype(jnp.bfloat16)
 

time: 51 us -> 49.8 us (0.976)
  blocking collectives: 45.3 us -> 43.9 us
    all_to_all x4, blocking collectives: 45.3 us -> 43.9 us  [exchange(): lax.all_to_all(blocks, ('gx', 'gy'), split_axis=0, concat_axis=0, tiled=T...]
where the time goes in v5:
time: 49.8 us; the launch traced here: 49.6 us
  blocking collectives  43.9 us (88%)
  Pallas kernels  3.98 us (8%)
  other arithmetic  0.8 us (2%)
  between operations  0.8 us (2%)
    all_to_all x4, blocking collectives, exchange(): lax.all_to_all(blocks, ('gx', 'gy'), split_axis=0, concat_axis=0, tiled=T...  43.9 us
    pallas_call x1, Pallas kernels, body(): pl.pallas_call(functools.partial(attend_kernel, row_groups), out_shape=bl...  1.89 us

profile of v5, /device:TPU:0, one launch (start us, length us, event | category | flops | bytes accessed | tf_op | source)
XLA Modules:
  0.0 49.6 jit_solution(4698183292385825903)
XLA Ops:
  0.0 0.0 copy-start
  0.0 0.0 copy-start.7
  0.7 0.0 copy-done
  0.8 0.0 copy-done.7
  0.8 0.0 copy-start.1
  0.8 0.0 copy-start.5
  0.8 0.0 copy-start.6
  0.8 0.2 shard_map.111
  1.0 15.3 %all_to_all.20.blocks_ref = bf16[32,16,128]{2,1,0:T(8,128)(2,1)S(1)} all-to-all(bf16[32,16,128]{2,1,0:T(8,128)(2,1)S(1)} %shard_map.111), channel_id=1, replica_groups=mesh['gx'=4,'gy'=8] {'gx','gy'}, dimensions={0} | all-to-all | bytes 262144 | tf_op jit(solution)/shard_map/all_to_all | solution.py:29
  16.3 0.0 copy-done.1
  16.3 0.0 copy-done.5
  16.3 0.0 copy-done.6
  16.3 0.0 copy-start.2
  16.3 0.0 copy-start.3
  16.3 0.0 copy-start.8
  16.3 0.0 copy-start.9
  16.4 1.0 %shard_map.112 = f32[320,128]{1,0:T(8,128)S(1)} custom-call(bf16[32,16,128]{2,1,0:T(8,128)(2,1)S(1)} %all_to_all.20.blocks_ref, bf16[2048,1024]{1,0:T(8,128)(2,1)S(1)} %copy-done.1, bf16[2048,128]{1,0:T(8,128)(2,1)S(1)} %copy-done.5, bf16[2048,128]{1,0:T(8,128)(2,1)S(1)} %copy-done.6), custom_call_target="tpu_custom_call" | custom-call | flops 20000000000 | tf_op jit(solution)/shard_map/pallas_call | solution.py:266
  17.4 9.6 %all_to_all.21 = f16[32,5,2,128]{3,2,1,0:T(2,128)(2,1)S(1)} all-to-all(f16[32,5,2,128]{3,2,1,0:T(2,128)(2,1)S(1)} %bitcast.24), channel_id=1, replica_groups=mesh['gx'=4,'gy'=8] {'gx','gy'}, dimensions={0} | all-to-all | bytes 163840 | tf_op jit(solution)/shard_map/all_to_all | solution.py:29
  27.0 0.1 convert_multiply_fusion
  27.0 0.0 copy-done.2
  27.0 0.0 copy-done.3
  27.0 0.0 copy-done.8
  27.1 0.0 copy-done.9
  27.1 0.0 copy-start.4
  27.1 1.9 %shard_map.113 = bf16[32,16,128]{2,1,0:T(8,128)(2,1)S(1)} custom-call(f32[8,128]{1,0:T(8,128)S(1)} %shard_map.110.turn_ref, f32[8,16]{1,0:T(8,128)S(1)} %bitcast.21, f32[8,16]{1,0:T(8,128)S(1)} %bitcast.22, f32[320,128]{1,0:T(8,128)S(1)} %bitcast.17, bf16[2048,1024]{1,0:T(8,128)(2,1)S(1)} %bitcast.18, bf16[2048,1024]{1,0:T(8,128)(2,1)S(1)} %bitcast.19), custom_call_target="tpu_custom_call" | custom-call | flops 20000000000 | tf_op jit(solution)/shard_map/pallas_call | solution.py:286
  29.0 9.9 %all_to_all.22.blocks_ref = bf16[32,16,128]{2,1,0:T(8,128)(2,1)S(1)} all-to-all(bf16[32,16,128]{2,1,0:T(8,128)(2,1)S(1)} %shard_map.113), channel_id=1, replica_groups=mesh['gx'=4,'gy'=8] {'gx','gy'}, dimensions={0} | all-to-all | bytes 262144 | tf_op jit(solution)/shard_map/all_to_all | solution.py:29
  38.9 0.0 copy-done.4
  38.9 0.8 %shard_map.114 = f32[256,128]{1,0:T(8,128)S(1)} custom-call(bf16[32,16,128]{2,1,0:T(8,128)(2,1)S(1)} %all_to_all.22.blocks_ref, bf16[2048,1024]{1,0:T(8,128)(2,1)S(1)} %copy-done.4), custom_call_target="tpu_custom_call" | custom-call | flops 20000000000 | tf_op jit(solution)/shard_map/pallas_call | solution.py:307
  39.8 9.1 %all_to_all.23 = f16[32,1,8,128]{3,2,1,0:T(8,128)(2,1)S(1)} all-to-all(f16[32,1,8,128]{3,2,1,0:T(8,128)(2,1)S(1)} %fusion), channel_id=1, replica_groups=mesh['gx'=4,'gy'=8] {'gx','gy'}, dimensions={0} | all-to-all | bytes 131072 | tf_op jit(solution)/shard_map/all_to_all | solution.py:29
  48.9 0.7 %add_convert_fusion = bf16[1,8192]{1,0:T(2,128)(2,1)} fusion(f32[1,8192]{1,0:T(1,128)S(1)} %bitcast.25, bf16[1,8192]{1,0:T(2,128)(2,1)S(1)} %copy-done), kind=kLoop, calls=%fused_computation.5 | loop fusion | flops 24576 | bytes 65536 | tf_op jit(solution)/shard_map/convert_element_type | solution.py:317
  (6 shorter events, 0.1 us)
Async XLA Ops:
  0.0 0.8 %copy-start = (bf16[1,8192]{1,0:T(2,128)(2,1)S(1)}, bf16[1,8192]{1,0:T(2,128)(2,1)}, u32[]{:S(2)}) copy-start(bf16[1,8192]{1,0:T(2,128)(2,1)} %hidden_ref.1) | copy-start | bytes 49156
  0.0 0.8 %copy-start.7 = (f32[8192]{0:T(1024)S(1)}, f32[8192]{0:T(1024)}, u32[]{:S(2)}) copy-start(f32[8192]{0:T(1024)} %param.12) | copy-start | bytes 98308
  0.8 15.5 %copy-start.1 = (bf16[2048,1024]{1,0:T(8,128)(2,1)S(1)}, bf16[2048,1024]{1,0:T(8,128)(2,1)}, u32[]{:S(2)}) copy-start(bf16[2048,1024]{1,0:T(8,128)(2,1)} %w_query_ref.1) | copy-start | bytes 12582916
  0.8 15.5 %copy-start.5 = (bf16[2048,128]{1,0:T(8,128)(2,1)S(1)}, bf16[2048,128]{1,0:T(8,128)(2,1)}, u32[]{:S(2)}) copy-start(bf16[2048,128]{1,0:T(8,128)(2,1)} %key_ref.1) | copy-start | bytes 1572868
  0.8 15.5 %copy-start.6 = (bf16[2048,128]{1,0:T(8,128)(2,1)S(1)}, bf16[2048,128]{1,0:T(8,128)(2,1)}, u32[]{:S(2)}) copy-start(bf16[2048,128]{1,0:T(8,128)(2,1)} %value_ref.1) | copy-start | bytes 1572868
  16.3 10.7 %copy-start.2 = (bf16[1,2048,1024]{2,1,0:T(8,128)(2,1)S(1)}, bf16[1,2048,1024]{2,1,0:T(8,128)(2,1)}, u32[]{:S(2)}) copy-start(bf16[1,2048,1024]{2,1,0:T(8,128)(2,1)} %param.17) | copy-start | bytes 12582916
  16.3 10.7 %copy-start.3 = (bf16[1,2048,1024]{2,1,0:T(8,128)(2,1)S(1)}, bf16[1,2048,1024]{2,1,0:T(8,128)(2,1)}, u32[]{:S(2)}) copy-start(bf16[1,2048,1024]{2,1,0:T(8,128)(2,1)} %param.18) | copy-start | bytes 12582916
  16.3 10.7 %copy-start.8 = (f32[1,16,8]{1,2,0:T(8,128)S(1)}, f32[1,16,8]{1,2,0:T(8,128)}, u32[]{:S(2)}) copy-start(f32[1,16,8]{1,2,0:T(8,128)} %param.19) | copy-start | bytes 1540
  16.3 10.7 %copy-start.9 = (f32[1,16,8]{1,2,0:T(8,128)S(1)}, f32[1,16,8]{1,2,0:T(8,128)}, u32[]{:S(2)}) copy-start(f32[1,16,8]{1,2,0:T(8,128)} %param.20) | copy-start | bytes 1540
  27.1 11.8 %copy-start.4 = (bf16[2048,1024]{1,0:T(8,128)(2,1)S(1)}, bf16[2048,1024]{1,0:T(8,128)(2,1)}, u32[]{:S(2)}) copy-start(bf16[2048,1024]{1,0:T(8,128)(2,1)} %weight_ref.1) | copy-start | bytes 12582916

commit v6 on v5

--- a/solution.py
+++ b/solution.py
@@ -85,7 +85,11 @@
     return jnp.concatenate([blocks_ref[:, k, :] for k in range(blocks_ref.shape[1])], axis=1)
 
 
-def send_rows(products, out_ref):
+def spaced(requests, count):
+    return pltpu.VMEM(((requests + 1) * count, LANES), jnp.float32)
+
+
+def send_rows(products, out_ref, spaced_ref):
     requests = products[0].shape[0]
     count = out_ref.shape[0] // requests
     parts = [
@@ -94,10 +98,11 @@
         for start in range(0, product.shape[1], LANES)
     ]
     for n, part in enumerate(parts):
-        out_ref[pl.ds(n, requests, stride=count), :] = part
-
-
-def project_kernel(blocks_ref, w_query_ref, key_ref, value_ref, out_ref):
+        spaced_ref[pl.ds(n, requests, stride=count), :] = part
+    out_ref[...] = spaced_ref[: requests * count, :]
+
+
+def project_kernel(blocks_ref, w_query_ref, key_ref, value_ref, out_ref, spaced_ref):
     rows = flat_rows(blocks_ref)
     products = [
         jnp.dot(rows, ref[...], preferred_element_type=jnp.float32)
@@ -105,12 +110,13 @@
     ]
     if products[1].shape[1] % LANES:
         products[1:] = [jnp.concatenate(products[1:], axis=1)]
-    send_rows(products, out_ref)
-
-
-def output_kernel(blocks_ref, weight_ref, out_ref):
+    send_rows(products, out_ref, spaced_ref)
+
+
+def output_kernel(blocks_ref, weight_ref, out_ref, spaced_ref):
     rows = flat_rows(blocks_ref)
-    send_rows([jnp.dot(rows, weight_ref[...], preferred_element_type=jnp.float32)], out_ref)
+    product = jnp.dot(rows, weight_ref[...], preferred_element_type=jnp.float32)
+    send_rows([product], out_ref, spaced_ref)
 
 
 def attend_kernel(
@@ -268,6 +274,7 @@
         out_shape=jax.ShapeDtypeStruct((devices * sent_rows, LANES), jnp.float32),
         in_specs=[VMEM] * 4,
         out_specs=VMEM,
+        scratch_shapes=[spaced(devices, sent_rows)],
         compiler_params=PARAMS,
         cost_estimate=COST,
     )(exchange(blocks), in_vmem(w_query), in_vmem(key_weight), in_vmem(value_weight))
@@ -309,6 +316,7 @@
         out_shape=jax.ShapeDtypeStruct((devices * out_rows, LANES), jnp.float32),
         in_specs=[VMEM] * 2,
         out_specs=VMEM,
+        scratch_shapes=[spaced(devices, out_rows)],
         compiler_params=PARAMS,
         cost_estimate=COST,
     )(exchange(attended), in_vmem(w_output))

time: 49.8 us -> 49.8 us (level)
  no operation moved by 1% of the time
where the time goes in v6:
time: 49.8 us; the launch traced here: 49.6 us
  blocking collectives  43.9 us (88%)
  Pallas kernels  4.01 us (8%)
  between operations  0.8 us (2%)
  other arithmetic  0.79 us (2%)
    all_to_all x4, blocking collectives, exchange(): lax.all_to_all(blocks, ('gx', 'gy'), split_axis=0, concat_axis=0, tiled=T...  43.9 us
    pallas_call x1, Pallas kernels, body(): pl.pallas_call(functools.partial(attend_kernel, row_groups), out_shape=bl...  1.89 us
    pallas_call x1, Pallas kernels, body(): pl.pallas_call(project_kernel, out_shape=jax.ShapeDtypeStruct((devices *...  1.01 us

profile of v6, /device:TPU:0, one launch (start us, length us, event | category | flops | bytes accessed | tf_op | source)
XLA Modules:
  0.0 49.6 jit_solution(16241582332398422362)
XLA Ops:
  0.0 0.0 copy-start
  0.0 0.0 copy-start.7
  0.7 0.0 copy-done
  0.8 0.0 copy-done.7
  0.8 0.0 copy-start.1
  0.8 0.0 copy-start.5
  0.8 0.0 copy-start.6
  0.8 0.2 shard_map.111
  1.0 15.3 %all_to_all.20.blocks_ref = bf16[32,16,128]{2,1,0:T(8,128)(2,1)S(1)} all-to-all(bf16[32,16,128]{2,1,0:T(8,128)(2,1)S(1)} %shard_map.111), channel_id=1, replica_groups=mesh['gx'=4,'gy'=8] {'gx','gy'}, dimensions={0} | all-to-all | bytes 262144 | tf_op jit(solution)/shard_map/all_to_all | solution.py:29
  16.3 0.0 copy-done.1
  16.3 0.0 copy-done.5
  16.3 0.0 copy-done.6
  16.3 0.0 copy-start.2
  16.3 0.0 copy-start.3
  16.3 0.0 copy-start.8
  16.3 0.0 copy-start.9
  16.4 1.0 %shard_map.112 = f32[320,128]{1,0:T(8,128)S(1)} custom-call(bf16[32,16,128]{2,1,0:T(8,128)(2,1)S(1)} %all_to_all.20.blocks_ref, bf16[2048,1024]{1,0:T(8,128)(2,1)S(1)} %copy-done.1, bf16[2048,128]{1,0:T(8,128)(2,1)S(1)} %copy-done.5, bf16[2048,128]{1,0:T(8,128)(2,1)S(1)} %copy-done.6), custom_call_target="tpu_custom_call" | custom-call | flops 20000000000 | tf_op jit(solution)/shard_map/pallas_call | solution.py:272
  17.4 9.6 %all_to_all.21 = f16[32,5,2,128]{3,2,1,0:T(2,128)(2,1)S(1)} all-to-all(f16[32,5,2,128]{3,2,1,0:T(2,128)(2,1)S(1)} %bitcast.24), channel_id=1, replica_groups=mesh['gx'=4,'gy'=8] {'gx','gy'}, dimensions={0} | all-to-all | bytes 163840 | tf_op jit(solution)/shard_map/all_to_all | solution.py:29
  27.0 0.1 convert_multiply_fusion
  27.0 0.0 copy-done.2
  27.1 0.0 copy-done.3
  27.1 0.0 copy-done.8
  27.1 0.0 copy-done.9
  27.1 0.0 copy-start.4
  27.1 1.9 %shard_map.113 = bf16[32,16,128]{2,1,0:T(8,128)(2,1)S(1)} custom-call(f32[8,128]{1,0:T(8,128)S(1)} %shard_map.110.turn_ref, f32[8,16]{1,0:T(8,128)S(1)} %bitcast.21, f32[8,16]{1,0:T(8,128)S(1)} %bitcast.22, f32[320,128]{1,0:T(8,128)S(1)} %bitcast.17, bf16[2048,1024]{1,0:T(8,128)(2,1)S(1)} %bitcast.18, bf16[2048,1024]{1,0:T(8,128)(2,1)S(1)} %bitcast.19), custom_call_target="tpu_custom_call" | custom-call | flops 20000000000 | tf_op jit(solution)/shard_map/pallas_call | solution.py:293
  29.0 9.9 %all_to_all.22.blocks_ref = bf16[32,16,128]{2,1,0:T(8,128)(2,1)S(1)} all-to-all(bf16[32,16,128]{2,1,0:T(8,128)(2,1)S(1)} %shard_map.113), channel_id=1, replica_groups=mesh['gx'=4,'gy'=8] {'gx','gy'}, dimensions={0} | all-to-all | bytes 262144 | tf_op jit(solution)/shard_map/all_to_all | solution.py:29
  38.9 0.0 copy-done.4
  38.9 0.9 %shard_map.114 = f32[256,128]{1,0:T(8,128)S(1)} custom-call(bf16[32,16,128]{2,1,0:T(8,128)(2,1)S(1)} %all_to_all.22.blocks_ref, bf16[2048,1024]{1,0:T(8,128)(2,1)S(1)} %copy-done.4), custom_call_target="tpu_custom_call" | custom-call | flops 20000000000 | tf_op jit(solution)/shard_map/pallas_call | solution.py:314
  39.8 9.1 %all_to_all.23 = f16[32,1,8,128]{3,2,1,0:T(8,128)(2,1)S(1)} all-to-all(f16[32,1,8,128]{3,2,1,0:T(8,128)(2,1)S(1)} %fusion), channel_id=1, replica_groups=mesh['gx'=4,'gy'=8] {'gx','gy'}, dimensions={0} | all-to-all | bytes 131072 | tf_op jit(solution)/shard_map/all_to_all | solution.py:29
  49.0 0.7 %add_convert_fusion = bf16[1,8192]{1,0:T(2,128)(2,1)} fusion(f32[1,8192]{1,0:T(1,128)S(1)} %bitcast.25, bf16[1,8192]{1,0:T(2,128)(2,1)S(1)} %copy-done), kind=kLoop, calls=%fused_computation.5 | loop fusion | flops 24576 | bytes 65536 | tf_op jit(solution)/shard_map/convert_element_type | solution.py:325
  (6 shorter events, 0.1 us)
Async XLA Ops:
  0.0 0.8 %copy-start = (bf16[1,8192]{1,0:T(2,128)(2,1)S(1)}, bf16[1,8192]{1,0:T(2,128)(2,1)}, u32[]{:S(2)}) copy-start(bf16[1,8192]{1,0:T(2,128)(2,1)} %hidden_ref.1) | copy-start | bytes 49156
  0.0 0.8 %copy-start.7 = (f32[8192]{0:T(1024)S(1)}, f32[8192]{0:T(1024)}, u32[]{:S(2)}) copy-start(f32[8192]{0:T(1024)} %param.12) | copy-start | bytes 98308
  0.8 15.5 %copy-start.1 = (bf16[2048,1024]{1,0:T(8,128)(2,1)S(1)}, bf16[2048,1024]{1,0:T(8,128)(2,1)}, u32[]{:S(2)}) copy-start(bf16[2048,1024]{1,0:T(8,128)(2,1)} %w_query_ref.1) | copy-start | bytes 12582916
  0.8 15.5 %copy-start.5 = (bf16[2048,128]{1,0:T(8,128)(2,1)S(1)}, bf16[2048,128]{1,0:T(8,128)(2,1)}, u32[]{:S(2)}) copy-start(bf16[2048,128]{1,0:T(8,128)(2,1)} %key_ref.1) | copy-start | bytes 1572868
  0.8 15.5 %copy-start.6 = (bf16[2048,128]{1,0:T(8,128)(2,1)S(1)}, bf16[2048,128]{1,0:T(8,128)(2,1)}, u32[]{:S(2)}) copy-start(bf16[2048,128]{1,0:T(8,128)(2,1)} %value_ref.1) | copy-start | bytes 1572868
  16.3 10.7 %copy-start.2 = (bf16[1,2048,1024]{2,1,0:T(8,128)(2,1)S(1)}, bf16[1,2048,1024]{2,1,0:T(8,128)(2,1)}, u32[]{:S(2)}) copy-start(bf16[1,2048,1024]{2,1,0:T(8,128)(2,1)} %param.17) | copy-start | bytes 12582916
  16.3 10.7 %copy-start.3 = (bf16[1,2048,1024]{2,1,0:T(8,128)(2,1)S(1)}, bf16[1,2048,1024]{2,1,0:T(8,128)(2,1)}, u32[]{:S(2)}) copy-start(bf16[1,2048,1024]{2,1,0:T(8,128)(2,1)} %param.18) | copy-start | bytes 12582916
  16.3 10.7 %copy-start.8 = (f32[1,16,8]{1,2,0:T(8,128)S(1)}, f32[1,16,8]{1,2,0:T(8,128)}, u32[]{:S(2)}) copy-start(f32[1,16,8]{1,2,0:T(8,128)} %param.19) | copy-start | bytes 1540
  16.3 10.7 %copy-start.9 = (f32[1,16,8]{1,2,0:T(8,128)S(1)}, f32[1,16,8]{1,2,0:T(8,128)}, u32[]{:S(2)}) copy-start(f32[1,16,8]{1,2,0:T(8,128)} %param.20) | copy-start | bytes 1540
  27.1 11.8 %copy-start.4 = (bf16[2048,1024]{1,0:T(8,128)(2,1)S(1)}, bf16[2048,1024]{1,0:T(8,128)(2,1)}, u32[]{:S(2)}) copy-start(bf16[2048,1024]{1,0:T(8,128)(2,1)} %weight_ref.1) | copy-start | bytes 12582916

commit v7 on v6

--- a/solution.py
+++ b/solution.py
@@ -21,20 +21,11 @@
 VMEM = pl.BlockSpec(memory_space=pltpu.VMEM)
 SMEM = pl.BlockSpec(memory_space=pltpu.SMEM)
 PARAMS = pltpu.CompilerParams(vmem_limit_bytes=4 * 1024 * 1024)
-SENT_SCALE = 16.0
 COST = pl.CostEstimate(flops=20_000_000_000, transcendentals=0, bytes_accessed=0)
 
 
 def exchange(blocks):
     return lax.all_to_all(blocks, ("gx", "gy"), split_axis=0, concat_axis=0, tiled=True)
-
-
-def exchange_sums(partial, devices):
-    sent = (partial * SENT_SCALE).astype(jnp.float16)
-    count = partial.shape[0] // devices
-    pair = 8 if count % 8 == 0 else 2 if count % 2 == 0 else 1
-    arrived = exchange(sent.reshape(devices, -1, pair, LANES)).reshape(partial.shape)
-    return arrived.astype(jnp.float32) * (1.0 / SENT_SCALE)
 
 
 def in_vmem(array):
@@ -99,7 +90,7 @@
     ]
     for n, part in enumerate(parts):
         spaced_ref[pl.ds(n, requests, stride=count), :] = part
-    out_ref[...] = spaced_ref[: requests * count, :]
+    out_ref[...] = spaced_ref[: requests * count, :].astype(out_ref.dtype)
 
 
 def project_kernel(blocks_ref, w_query_ref, key_ref, value_ref, out_ref, spaced_ref):
@@ -278,7 +269,7 @@
         compiler_params=PARAMS,
         cost_estimate=COST,
     )(exchange(blocks), in_vmem(w_query), in_vmem(key_weight), in_vmem(value_weight))
-    sums = exchange_sums(partial, devices)
+    sums = exchange(partial.reshape(devices, sent_rows, 1, LANES))
     if key_cols != HEAD_SIZE:
         sums = sums.reshape(row_groups, column_groups, sent_rows * LANES)
         sums = jnp.concatenate(
@@ -313,14 +304,14 @@
     out_rows = out_cols // LANES
     partial = pl.pallas_call(
         output_kernel,
-        out_shape=jax.ShapeDtypeStruct((devices * out_rows, LANES), jnp.float32),
+        out_shape=jax.ShapeDtypeStruct((devices * out_rows, LANES), jnp.bfloat16),
         in_specs=[VMEM] * 2,
         out_specs=VMEM,
         scratch_shapes=[spaced(devices, out_rows)],
         compiler_params=PARAMS,
         cost_estimate=COST,
     )(exchange(attended), in_vmem(w_output))
-    update = exchange_sums(partial, devices)
+    update = exchange(partial.reshape(devices, out_rows, LANES)).astype(jnp.float32)
     update = jnp.sum(update.reshape(row_groups, column_groups * out_rows, LANES), axis=0)
     return (hidden_in.astype(jnp.float32) + update.reshape(1, width)).astype(jnp.bfloat16)
 

time: 49.8 us -> 51 us (1.024)
  blocking collectives: 43.9 us -> 45.3 us
    all_to_all x4, blocking collectives: 43.9 us -> 45.3 us  [exchange(): lax.all_to_all(blocks, ('gx', 'gy'), split_axis=0, concat_axis=0, tiled=T...]
where the time goes in v7:
time: 51 us; the launch traced here: 50.8 us
  blocking collectives  45.3 us (89%)
  Pallas kernels  4.01 us (8%)
  between operations  0.75 us (1%)
  other arithmetic  0.67 us (1%)
    all_to_all x4, blocking collectives, exchange(): lax.all_to_all(blocks, ('gx', 'gy'), split_axis=0, concat_axis=0, tiled=T...  45.3 us
    pallas_call x1, Pallas kernels, body(): pl.pallas_call(functools.partial(attend_kernel, row_groups), out_shape=bl...  1.89 us

profile of v7, /device:TPU:0, one launch (start us, length us, event | category | flops | bytes accessed | tf_op | source)
XLA Modules:
  0.0 50.8 jit_solution(17835089953847600673)
XLA Ops:
  0.0 0.0 copy-start
  0.0 0.0 copy-start.7
  0.7 0.0 copy-done
  0.8 0.0 copy-done.7
  0.8 0.0 copy-start.1
  0.8 0.0 copy-start.5
  0.8 0.0 copy-start.6
  0.8 0.2 shard_map.111
  1.0 15.3 %all_to_all.20.blocks_ref = bf16[32,16,128]{2,1,0:T(8,128)(2,1)S(1)} all-to-all(bf16[32,16,128]{2,1,0:T(8,128)(2,1)S(1)} %shard_map.111), channel_id=1, replica_groups=mesh['gx'=4,'gy'=8] {'gx','gy'}, dimensions={0} | all-to-all | bytes 262144 | tf_op jit(solution)/shard_map/all_to_all | solution.py:28
  16.3 0.0 copy-done.1
  16.3 0.0 copy-done.5
  16.3 0.0 copy-done.6
  16.3 0.0 copy-start.2
  16.3 0.0 copy-start.3
  16.3 0.0 copy-start.8
  16.3 0.0 copy-start.9
  16.4 1.0 %shard_map.112 = f32[320,128]{1,0:T(8,128)S(1)} custom-call(bf16[32,16,128]{2,1,0:T(8,128)(2,1)S(1)} %all_to_all.20.blocks_ref, bf16[2048,1024]{1,0:T(8,128)(2,1)S(1)} %copy-done.1, bf16[2048,128]{1,0:T(8,128)(2,1)S(1)} %copy-done.5, bf16[2048,128]{1,0:T(8,128)(2,1)S(1)} %copy-done.6), custom_call_target="tpu_custom_call" | custom-call | flops 20000000000 | tf_op jit(solution)/shard_map/pallas_call | solution.py:263
  17.4 10.5 %all_to_all.21 = f32[32,10,1,128]{3,2,1,0:T(1,128)S(1)} all-to-all(f32[32,10,1,128]{3,2,1,0:T(1,128)S(1)} %bitcast.18), channel_id=1, replica_groups=mesh['gx'=4,'gy'=8] {'gx','gy'}, dimensions={0} | all-to-all | bytes 327680 | tf_op jit(solution)/shard_map/all_to_all | solution.py:28
  27.9 0.0 copy-done.2
  27.9 0.0 copy-done.3
  27.9 0.0 copy-done.8
  27.9 0.0 copy-done.9
  27.9 0.0 copy-start.4
  28.0 1.9 %shard_map.113 = bf16[32,16,128]{2,1,0:T(8,128)(2,1)S(1)} custom-call(f32[8,128]{1,0:T(8,128)S(1)} %shard_map.110.turn_ref, f32[8,16]{1,0:T(8,128)S(1)} %bitcast.23, f32[8,16]{1,0:T(8,128)S(1)} %bitcast.24, f32[320,128]{1,0:T(8,128)S(1)} %bitcast.17, bf16[2048,1024]{1,0:T(8,128)(2,1)S(1)} %bitcast.20, bf16[2048,1024]{1,0:T(8,128)(2,1)S(1)} %bitcast.21), custom_call_target="tpu_custom_call" | custom-call | flops 20000000000 | tf_op jit(solution)/shard_map/pallas_call | solution.py:284
  29.8 10.3 %all_to_all.22.blocks_ref = bf16[32,16,128]{2,1,0:T(8,128)(2,1)S(1)} all-to-all(bf16[32,16,128]{2,1,0:T(8,128)(2,1)S(1)} %shard_map.113), channel_id=1, replica_groups=mesh['gx'=4,'gy'=8] {'gx','gy'}, dimensions={0} | all-to-all | bytes 262144 | tf_op jit(solution)/shard_map/all_to_all | solution.py:28
  40.1 0.0 copy-done.4
  40.1 0.9 %shard_map.114 = bf16[256,128]{1,0:T(8,128)(2,1)S(1)} custom-call(bf16[32,16,128]{2,1,0:T(8,128)(2,1)S(1)} %all_to_all.22.blocks_ref, bf16[2048,1024]{1,0:T(8,128)(2,1)S(1)} %copy-done.4), custom_call_target="tpu_custom_call" | custom-call | flops 20000000000 | tf_op jit(solution)/shard_map/pallas_call | solution.py:305
  41.0 9.2 %all_to_all.23 = bf16[32,8,128]{2,1,0:T(8,128)(2,1)S(1)} all-to-all(bf16[32,8,128]{2,1,0:T(8,128)(2,1)S(1)} %bitcast.19), channel_id=1, replica_groups=mesh['gx'=4,'gy'=8] {'gx','gy'}, dimensions={0} | all-to-all | bytes 131072 | tf_op jit(solution)/shard_map/all_to_all | solution.py:28
  50.2 0.7 %add_convert_fusion = bf16[1,8192]{1,0:T(2,128)(2,1)} fusion(f32[1,8192]{1,0:T(1,128)S(1)} %bitcast.26, bf16[1,8192]{1,0:T(2,128)(2,1)S(1)} %copy-done), kind=kLoop, calls=%fused_computation.1 | loop fusion | flops 24576 | bytes 65536 | tf_op jit(solution)/shard_map/convert_element_type | solution.py:316
  (3 shorter events, 0.1 us)
Async XLA Ops:
  0.0 0.8 %copy-start = (bf16[1,8192]{1,0:T(2,128)(2,1)S(1)}, bf16[1,8192]{1,0:T(2,128)(2,1)}, u32[]{:S(2)}) copy-start(bf16[1,8192]{1,0:T(2,128)(2,1)} %hidden_ref.1) | copy-start | bytes 49156
  0.0 0.8 %copy-start.7 = (f32[8192]{0:T(1024)S(1)}, f32[8192]{0:T(1024)}, u32[]{:S(2)}) copy-start(f32[8192]{0:T(1024)} %param.12) | copy-start | bytes 98308
  0.8 15.5 %copy-start.1 = (bf16[2048,1024]{1,0:T(8,128)(2,1)S(1)}, bf16[2048,1024]{1,0:T(8,128)(2,1)}, u32[]{:S(2)}) copy-start(bf16[2048,1024]{1,0:T(8,128)(2,1)} %w_query_ref.1) | copy-start | bytes 12582916
  0.8 15.5 %copy-start.5 = (bf16[2048,128]{1,0:T(8,128)(2,1)S(1)}, bf16[2048,128]{1,0:T(8,128)(2,1)}, u32[]{:S(2)}) copy-start(bf16[2048,128]{1,0:T(8,128)(2,1)} %key_ref.1) | copy-start | bytes 1572868
  0.8 15.5 %copy-start.6 = (bf16[2048,128]{1,0:T(8,128)(2,1)S(1)}, bf16[2048,128]{1,0:T(8,128)(2,1)}, u32[]{:S(2)}) copy-start(bf16[2048,128]{1,0:T(8,128)(2,1)} %value_ref.1) | copy-start | bytes 1572868
  16.3 11.6 %copy-start.2 = (bf16[1,2048,1024]{2,1,0:T(8,128)(2,1)S(1)}, bf16[1,2048,1024]{2,1,0:T(8,128)(2,1)}, u32[]{:S(2)}) copy-start(bf16[1,2048,1024]{2,1,0:T(8,128)(2,1)} %param.17) | copy-start | bytes 12582916
  16.3 11.6 %copy-start.3 = (bf16[1,2048,1024]{2,1,0:T(8,128)(2,1)S(1)}, bf16[1,2048,1024]{2,1,0:T(8,128)(2,1)}, u32[]{:S(2)}) copy-start(bf16[1,2048,1024]{2,1,0:T(8,128)(2,1)} %param.18) | copy-start | bytes 12582916
  16.3 11.6 %copy-start.8 = (f32[1,16,8]{1,2,0:T(8,128)S(1)}, f32[1,16,8]{1,2,0:T(8,128)}, u32[]{:S(2)}) copy-start(f32[1,16,8]{1,2,0:T(8,128)} %param.19) | copy-start | bytes 1540
  16.3 11.6 %copy-start.9 = (f32[1,16,8]{1,2,0:T(8,128)S(1)}, f32[1,16,8]{1,2,0:T(8,128)}, u32[]{:S(2)}) copy-start(f32[1,16,8]{1,2,0:T(8,128)} %param.20) | copy-start | bytes 1540
  27.9 12.2 %copy-start.4 = (bf16[2048,1024]{1,0:T(8,128)(2,1)S(1)}, bf16[2048,1024]{1,0:T(8,128)(2,1)}, u32[]{:S(2)}) copy-start(bf16[2048,1024]{1,0:T(8,128)(2,1)} %weight_ref.1) | copy-start | bytes 12582916

commit v8 on v7

--- a/solution.py
+++ b/solution.py
@@ -51,13 +51,9 @@
     turn_ref[2:3, :] = jnp.full((1, HEAD_SIZE), length)
 
 
-def norm_kernel(row_groups, turn_ref, hidden_ref, gain_ref, blocks_ref, wide_ref):
-    rows = wide_ref.shape[0]
-    for row in range(rows):
-        wide_ref[row : row + 1, :] = hidden_ref[:, row * LANES : (row + 1) * LANES].astype(
-            jnp.float32
-        )
-    wide = wide_ref[...]
+def norm_kernel(row_groups, turn_ref, hidden_ref, gain_ref, blocks_ref):
+    rows = gain_ref.shape[0]
+    wide = hidden_ref[...].astype(jnp.float32).reshape(rows, LANES)
     variance = jnp.sum(wide * wide, keepdims=True) * (1.0 / (rows * LANES))
     normed = (wide * lax.rsqrt(variance + NORM_EPS) * gain_ref[...]).astype(jnp.bfloat16)
     spread_blocks(normed, row_groups, blocks_ref)
@@ -254,7 +250,6 @@
         out_shape=blocks_type,
         in_specs=[VMEM] * 3,
         out_specs=VMEM,
-        scratch_shapes=[pltpu.VMEM((width // LANES, LANES), jnp.float32)],
         compiler_params=PARAMS,
         cost_estimate=COST,
     )(turn, in_vmem(hidden_in), in_vmem(norm_gain.reshape(-1, LANES)))
@@ -269,7 +264,8 @@
         compiler_params=PARAMS,
         cost_estimate=COST,
     )(exchange(blocks), in_vmem(w_query), in_vmem(key_weight), in_vmem(value_weight))
-    sums = exchange(partial.reshape(devices, sent_rows, 1, LANES))
+    pair = 2 if sent_rows % 2 == 0 else 1
+    sums = exchange(partial.reshape(devices, sent_rows // pair, pair, LANES))
     if key_cols != HEAD_SIZE:
         sums = sums.reshape(row_groups, column_groups, sent_rows * LANES)
         sums = jnp.concatenate(

time: 51 us -> 51 us (level)
  no operation moved by 1% of the time
where the time goes in v8:
time: 51 us; the launch traced here: 50.8 us
  blocking collectives  45.3 us (89%)
  Pallas kernels  3.99 us (8%)
  between operations  0.75 us (1%)
  other arithmetic  0.67 us (1%)
    all_to_all x4, blocking collectives, exchange(): lax.all_to_all(blocks, ('gx', 'gy'), split_axis=0, concat_axis=0, tiled=T...  45.3 us
    pallas_call x1, Pallas kernels, body(): pl.pallas_call(functools.partial(attend_kernel, row_groups), out_shape=bl...  1.89 us

profile of v8, /device:TPU:0, one launch (start us, length us, event | category | flops | bytes accessed | tf_op | source)
XLA Modules:
  0.0 50.8 jit_solution(6864822860292382914)
XLA Ops:
  0.0 0.0 copy-start
  0.0 0.0 copy-start.7
  0.7 0.0 copy-done
  0.8 0.0 copy-done.7
  0.8 0.0 copy-start.1
  0.8 0.0 copy-start.5
  0.8 0.0 copy-start.6
  0.8 0.1 shard_map.111
  0.9 15.3 %all_to_all.20.blocks_ref = bf16[32,16,128]{2,1,0:T(8,128)(2,1)S(1)} all-to-all(bf16[32,16,128]{2,1,0:T(8,128)(2,1)S(1)} %shard_map.111), channel_id=1, replica_groups=mesh['gx'=4,'gy'=8] {'gx','gy'}, dimensions={0} | all-to-all | bytes 262144 | tf_op jit(solution)/shard_map/all_to_all | solution.py:28
  16.3 0.0 copy-done.1
  16.3 0.0 copy-done.5
  16.3 0.0 copy-done.6
  16.3 0.0 copy-start.2
  16.3 0.0 copy-start.3
  16.3 0.0 copy-start.8
  16.3 0.0 copy-start.9
  16.3 1.0 %shard_map.112 = f32[320,128]{1,0:T(8,128)S(1)} custom-call(bf16[32,16,128]{2,1,0:T(8,128)(2,1)S(1)} %all_to_all.20.blocks_ref, bf16[2048,1024]{1,0:T(8,128)(2,1)S(1)} %copy-done.1, bf16[2048,128]{1,0:T(8,128)(2,1)S(1)} %copy-done.5, bf16[2048,128]{1,0:T(8,128)(2,1)S(1)} %copy-done.6), custom_call_target="tpu_custom_call" | custom-call | flops 20000000000 | tf_op jit(solution)/shard_map/pallas_call | solution.py:258
  17.4 10.5 %all_to_all.21 = f32[32,5,2,128]{3,2,1,0:T(2,128)S(1)} all-to-all(f32[32,5,2,128]{3,2,1,0:T(2,128)S(1)} %bitcast.18), channel_id=1, replica_groups=mesh['gx'=4,'gy'=8] {'gx','gy'}, dimensions={0} | all-to-all | bytes 327680 | tf_op jit(solution)/shard_map/all_to_all | solution.py:28
  27.9 0.0 copy-done.2
  27.9 0.0 copy-done.3
  27.9 0.0 copy-done.8
  27.9 0.0 copy-done.9
  27.9 0.0 copy-start.4
  27.9 1.9 %shard_map.113 = bf16[32,16,128]{2,1,0:T(8,128)(2,1)S(1)} custom-call(f32[8,128]{1,0:T(8,128)S(1)} %shard_map.110.turn_ref, f32[8,16]{1,0:T(8,128)S(1)} %bitcast.23, f32[8,16]{1,0:T(8,128)S(1)} %bitcast.24, f32[320,128]{1,0:T(8,128)S(1)} %bitcast.17, bf16[2048,1024]{1,0:T(8,128)(2,1)S(1)} %bitcast.20, bf16[2048,1024]{1,0:T(8,128)(2,1)S(1)} %bitcast.21), custom_call_target="tpu_custom_call" | custom-call | flops 20000000000 | tf_op jit(solution)/shard_map/pallas_call | solution.py:280
  29.8 10.3 %all_to_all.22.blocks_ref = bf16[32,16,128]{2,1,0:T(8,128)(2,1)S(1)} all-to-all(bf16[32,16,128]{2,1,0:T(8,128)(2,1)S(1)} %shard_map.113), channel_id=1, replica_groups=mesh['gx'=4,'gy'=8] {'gx','gy'}, dimensions={0} | all-to-all | bytes 262144 | tf_op jit(solution)/shard_map/all_to_all | solution.py:28
  40.1 0.0 copy-done.4
  40.1 0.9 %shard_map.114 = bf16[256,128]{1,0:T(8,128)(2,1)S(1)} custom-call(bf16[32,16,128]{2,1,0:T(8,128)(2,1)S(1)} %all_to_all.22.blocks_ref, bf16[2048,1024]{1,0:T(8,128)(2,1)S(1)} %copy-done.4), custom_call_target="tpu_custom_call" | custom-call | flops 20000000000 | tf_op jit(solution)/shard_map/pallas_call | solution.py:301
  41.0 9.2 %all_to_all.23 = bf16[32,8,128]{2,1,0:T(8,128)(2,1)S(1)} all-to-all(bf16[32,8,128]{2,1,0:T(8,128)(2,1)S(1)} %bitcast.19), channel_id=1, replica_groups=mesh['gx'=4,'gy'=8] {'gx','gy'}, dimensions={0} | all-to-all | bytes 131072 | tf_op jit(solution)/shard_map/all_to_all | solution.py:28
  50.2 0.7 %add_convert_fusion = bf16[1,8192]{1,0:T(2,128)(2,1)} fusion(f32[1,8192]{1,0:T(1,128)S(1)} %bitcast.26, bf16[1,8192]{1,0:T(2,128)(2,1)S(1)} %copy-done), kind=kLoop, calls=%fused_computation.1 | loop fusion | flops 24576 | bytes 65536 | tf_op jit(solution)/shard_map/convert_element_type | solution.py:312
  (3 shorter events, 0.1 us)
Async XLA Ops:
  0.0 0.8 %copy-start = (bf16[1,8192]{1,0:T(2,128)(2,1)S(1)}, bf16[1,8192]{1,0:T(2,128)(2,1)}, u32[]{:S(2)}) copy-start(bf16[1,8192]{1,0:T(2,128)(2,1)} %hidden_ref.1) | copy-start | bytes 49156
  0.0 0.8 %copy-start.7 = (f32[8192]{0:T(1024)S(1)}, f32[8192]{0:T(1024)}, u32[]{:S(2)}) copy-start(f32[8192]{0:T(1024)} %param.12) | copy-start | bytes 98308
  0.8 15.5 %copy-start.1 = (bf16[2048,1024]{1,0:T(8,128)(2,1)S(1)}, bf16[2048,1024]{1,0:T(8,128)(2,1)}, u32[]{:S(2)}) copy-start(bf16[2048,1024]{1,0:T(8,128)(2,1)} %w_query_ref.1) | copy-start | bytes 12582916
  0.8 15.5 %copy-start.5 = (bf16[2048,128]{1,0:T(8,128)(2,1)S(1)}, bf16[2048,128]{1,0:T(8,128)(2,1)}, u32[]{:S(2)}) copy-start(bf16[2048,128]{1,0:T(8,128)(2,1)} %key_ref.1) | copy-start | bytes 1572868
  0.8 15.5 %copy-start.6 = (bf16[2048,128]{1,0:T(8,128)(2,1)S(1)}, bf16[2048,128]{1,0:T(8,128)(2,1)}, u32[]{:S(2)}) copy-start(bf16[2048,128]{1,0:T(8,128)(2,1)} %value_ref.1) | copy-start | bytes 1572868
  16.3 11.6 %copy-start.2 = (bf16[1,2048,1024]{2,1,0:T(8,128)(2,1)S(1)}, bf16[1,2048,1024]{2,1,0:T(8,128)(2,1)}, u32[]{:S(2)}) copy-start(bf16[1,2048,1024]{2,1,0:T(8,128)(2,1)} %param.17) | copy-start | bytes 12582916
  16.3 11.6 %copy-start.3 = (bf16[1,2048,1024]{2,1,0:T(8,128)(2,1)S(1)}, bf16[1,2048,1024]{2,1,0:T(8,128)(2,1)}, u32[]{:S(2)}) copy-start(bf16[1,2048,1024]{2,1,0:T(8,128)(2,1)} %param.18) | copy-start | bytes 12582916
  16.3 11.6 %copy-start.8 = (f32[1,16,8]{1,2,0:T(8,128)S(1)}, f32[1,16,8]{1,2,0:T(8,128)}, u32[]{:S(2)}) copy-start(f32[1,16,8]{1,2,0:T(8,128)} %param.19) | copy-start | bytes 1540
  16.3 11.6 %copy-start.9 = (f32[1,16,8]{1,2,0:T(8,128)S(1)}, f32[1,16,8]{1,2,0:T(8,128)}, u32[]{:S(2)}) copy-start(f32[1,16,8]{1,2,0:T(8,128)} %param.20) | copy-start | bytes 1540
  27.9 12.2 %copy-start.4 = (bf16[2048,1024]{1,0:T(8,128)(2,1)S(1)}, bf16[2048,1024]{1,0:T(8,128)(2,1)}, u32[]{:S(2)}) copy-start(bf16[2048,1024]{1,0:T(8,128)(2,1)} %weight_ref.1) | copy-start | bytes 12582916
